TPU v7x, 128 devices: a whole 4x4x4 slice. The times are simulated.
128 devices in a mesh: dp: 64 (over y, z, x), shard: 2 (over core).
Axes of the slice: x: 4, y: 4, z: 4, core: 2. Of those that a mesh axis runs over, the one named last changes fastest.
Arguments:
- tokens: bfloat16 [32768, 1024], P(('dp', 'shard')), may hold values from -24 to 24
- packed_proj: bfloat16 [1024, 3072], P(('dp', 'shard')), may hold values from -0.1875 to 0.1875
- mixer_proj: bfloat16 [1024, 1024], P(('dp', 'shard')), may hold values from -0.75 to 0.75
- expand_proj: bfloat16 [1024, 5248], P(('dp', 'shard')), may hold values from -0.1875 to 0.1875
- reduce_proj: bfloat16 [1024, 2624], P(('dp', 'shard')), may hold values from -0.125 to 0.125
- first_gain: bfloat16 [1024], P(('dp', 'shard')), may hold values from 0.25 to 1.75
- second_gain: bfloat16 [1024], P(('dp', 'shard')), may hold values from 0.25 to 1.75
- sequence_lengths: int32 [512], P(('dp', 'shard')), may hold values from 0 to 256, as said below
- cotangent: bfloat16 [32768, 1024], P(('dp', 'shard')), may hold values from -24 to 24
Outputs:
- block_output: bfloat16 [32768, 1024], P(('dp', 'shard'))
- input_grad: float32 [32768, 1024], P(('dp', 'shard'))
- packed_grad: float32 [1024, 3072], P(('dp', 'shard'))
- mixer_grad: float32 [1024, 1024], P(('dp', 'shard'))
- expand_grad: float32 [1024, 5248], P(('dp', 'shard'))
- reduce_grad: float32 [1024, 2624], P(('dp', 'shard'))
- first_gain_grad: float32 [1024], P(('dp', 'shard'))
- second_gain_grad: float32 [1024], P(('dp', 'shard'))
Inputs may be any that keep to these rules, and one draw needn't show every extreme that they name: `sequence_lengths`: each aligned group of 4 entries gives the sequences of one block of 256 slots in order; their sum is at most 256 and the block's remaining slots are padding. Lengths may be 0. In every draw one block holds a single sequence of 256 tokens.
All inputs are finite; a program needn't handle non-finite values.
Results may differ from a plain program's by a relative error of at most 0.019.
Values may be sent and summed in bfloat16 or wider, within the bound.
No kernel may reach another device: no remote copies, remote signals or barrier semaphores. Data moves between devices by JAX's collectives and lax.ppermute only.
A program may use at most 192 MiB of HBM per device.

v0:
```python
import functools

import jax
import jax.numpy as jnp
from jax import lax
from jax.experimental import pallas as pl
from jax.experimental.pallas import tpu as pltpu
from jax.sharding import Mesh
from jax.sharding import PartitionSpec as P

H = 16
HD = 64
PAIR = 2 * HD
PAIRS = H // 2
epsilon = 1e-05
rope_base = 160000.0
masked_score = -1e30
AXES = ("y", "z", "x")
ALL = ("y", "z", "x", "c")
VMEM = 60 * 1024 * 1024
bf16 = jnp.bfloat16
f32 = jnp.float32

D = 1024
FF = 2624
CHUNKS = 3
CW = 896
MIX_AT = 3 * D
GAIN_AT = 4 * D
FF_AT = 4 * D + 128
W_COLS = FF_AT + CHUNKS * 3 * CW
ROWS = 512
MIX_CUTS = ((0, 384), (384, 768), (768, 1024))
A_COLS = D + 384


def dot(a, b):
    return lax.dot_general(a, b, (((1,), (0,)), ((), ())), preferred_element_type=f32)


def dot_t(a, b):
    return lax.dot_general(a, b, (((1,), (1,)), ((), ())), preferred_element_type=f32)


def dot_first(a, b):
    return lax.dot_general(a, b, (((0,), (0,)), ((), ())), preferred_element_type=f32)


def norm_parts(values):
    centered = values - jnp.mean(values, axis=-1, keepdims=True)
    scale = lax.rsqrt(jnp.mean(centered * centered, axis=-1, keepdims=True) + epsilon)
    return centered * scale, scale


def half_swapped(v, low_half):
    return jnp.where(low_half, pltpu.roll(v, PAIR - HD // 2, 1), pltpu.roll(v, HD // 2, 1))


def pair_slice(p, at=0):
    return pl.ds(p * PAIR + at, PAIR)


def cotangent_kernel(cot_ref, seg_ref, *refs):
    perms, gt_ref, gtts = refs[:CHUNKS], refs[CHUNKS], refs[CHUNKS + 1 :]
    gt = jnp.where(seg_ref[...] < 4, cot_ref[...].astype(f32), 0.0).astype(bf16)
    gt_ref[...] = gt
    for perm, gtt in zip(perms, gtts):
        gtt[...] = dot_t(perm[...], gt).astype(bf16)


def attend_kernel(
    tok_ref, seg_ref, segt_ref, cos_ref, sin_ref, w_ref,
    qkv_hbm, prob_hbm, res_ref, h1_ref, h2_ref, mixed, gain_ref,
    wp, wm, wg, packed, bias, qkv, prob, sems, out_sems,
):
    copies = [
        pltpu.make_async_copy(w_ref.at[:, pl.ds(GAIN_AT, 128)], wg, sems.at[0]),
        pltpu.make_async_copy(w_ref.at[:, pl.ds(0, 3 * D)], wp, sems.at[1]),
        pltpu.make_async_copy(w_ref.at[:, pl.ds(MIX_AT, D)], wm, sems.at[2]),
    ]
    for c in copies:
        c.start()
    tokens = tok_ref[...].astype(f32)
    xhat, _ = norm_parts(tokens)
    bias[...] = jnp.where(seg_ref[...] == segt_ref[...], 0.0, masked_score)
    copies[0].wait()
    gains = jnp.transpose(wg[...].astype(f32))[:8]
    gain_ref[...] = gains
    h1 = (xhat * gains[0:1]).astype(bf16)
    h1_ref[...] = h1
    copies[1].wait()
    packed[...] = dot(h1, wp[...])
    low_half = lax.broadcasted_iota(jnp.int32, (1, PAIR), 1) % HD < HD // 2
    first = lax.broadcasted_iota(jnp.int32, (1, PAIR), 1) < HD
    zero = jnp.zeros((), bf16)

    def pair(p):
        cos, sin = cos_ref[...], sin_ref[...]
        q = packed[:, pair_slice(p)]
        k = packed[:, pair_slice(p, D)]
        q = (q * cos + half_swapped(q, low_half) * sin).astype(bf16)
        k = (k * cos + half_swapped(k, low_half) * sin).astype(bf16)
        v = packed[:, pair_slice(p, 2 * D)].astype(bf16)
        qkv[:, pair_slice(p)] = q
        qkv[:, pair_slice(p, D)] = k
        qkv[:, pair_slice(p, 2 * D)] = v
        outs = []
        for side in range(2):
            mine = first if side == 0 else jnp.logical_not(first)
            scores = dot_t(jnp.where(mine, q, zero), k) * (HD**-0.5) + bias[...]
            top = jnp.max(scores, axis=-1, keepdims=True)
            e = jnp.exp(scores - top)
            probs = e * (1.0 / jnp.sum(e, axis=-1, keepdims=True))
            prob[2 * p + side] = probs
            outs.append(dot(probs.astype(bf16), v))
        mixed[:, pair_slice(p)] = jnp.where(first, outs[0], outs[1]).astype(bf16)

    outs = []
    for i in range(2):
        for p in range(i * PAIRS // 2, (i + 1) * PAIRS // 2):
            pair(p)
        part = pl.ds(i * PAIRS, PAIRS)
        outs.append(pltpu.make_async_copy(prob.at[part], prob_hbm.at[part], out_sems.at[i]))
        outs[-1].start()
    outs.append(pltpu.make_async_copy(qkv, qkv_hbm, out_sems.at[2]))
    outs[-1].start()
    copies[2].wait()
    residual = tokens + dot(mixed[...], wm[...])
    res_ref[...] = residual
    xhat2, _ = norm_parts(residual)
    h2_ref[...] = (xhat2 * gains[1:2]).astype(bf16)
    for c in outs:
        c.wait()


def started(pairs, sems):
    copies = [pltpu.make_async_copy(a, b, sems.at[i]) for i, (a, b) in enumerate(pairs)]
    for c in copies:
        c.start()
    return copies


def in_part_order(order_ref, part, rows, tmp):
    for r in range(D // 8):
        at = pl.multiple_of(order_ref[part * (D // 8) + r], 8)
        tmp[pl.ds(8 * r, 8), :] = rows[pl.ds(at, 8), :]
    return tmp[...].astype(bf16)


def gated_kernel(
    order_ref, h2_hbm, gt_hbm, gtt0, gtt1, gtt2, w_hbm,
    branch_ref, gh2_ref, sib0, sib1, sib2, own0, own1, own2,
    h2, gt, gtt, w, gate, up, gh, hid, gg, gu, turned, tmp, h2t, grads, sems, out_sems,
):
    pairs = [(h2_hbm, h2)]
    for j, g in enumerate((gtt0, gtt1, gtt2)):
        base = FF_AT + j * 3 * CW
        pairs += [
            (w_hbm.at[:, pl.ds(base + i * CW, CW)], w.at[j, :, pl.ds(i * CW, CW)]) for i in range(3)
        ]
        pairs.append((g, gtt.at[j]))
        if j == 0:
            pairs.append((gt_hbm, gt))
    copies = iter(started(pairs, sems))
    next(copies).wait()
    size = 16

    def rows(i, carry):
        r = pl.ds(pl.multiple_of(i * size, size), size)
        g, u, d = gate[r, :], up[r, :], gh[r, :]
        cdf = 0.5 * (1.0 + lax.erf(g * (0.5**0.5)))
        act = g * cdf
        slope = cdf + g * (jnp.exp(-0.5 * g * g) * 0.3989422804014327)
        hid[r, :] = (act * u).astype(bf16)
        gg[r, :] = (d * u * slope).astype(bf16)
        gu[r, :] = (d * act).astype(bf16)
        return carry

    outs = []
    for j, targets in enumerate(((sib0, own0), (sib1, own1), (sib2, own2))):
        next(copies).wait()
        gate[...] = dot(h2[...], w[j, :, :CW])
        next(copies).wait()
        up[...] = dot(h2[...], w[j, :, CW : 2 * CW])
        for _ in range(3 if j == 0 else 2):
            next(copies).wait()
        gh[...] = dot(gt[...], w[j, :, 2 * CW :])
        if j == 0:
            turned[...] = jnp.transpose(h2[...].astype(f32))
        h2t[...] = in_part_order(order_ref, j, turned, tmp)
        lax.fori_loop(0, gate.shape[0] // size, rows, 0)
        for half, to in enumerate(targets):
            rows_at = pl.ds(half * ROWS, ROWS)
            for i, (left, right) in enumerate(((h2t, gg), (h2t, gu), (gtt.at[j], hid))):
                cols = pl.ds(i * CW, CW)
                grads[j, rows_at, cols] = dot(left[rows_at, :], right[...]).astype(bf16)
                outs.append(
                    pltpu.make_async_copy(
                        grads.at[j, rows_at, cols], to.at[:, cols], out_sems.at[6 * j + 3 * half + i]
                    )
                )
                outs[-1].start()
        more = dot_t(hid[...], w[j, :, 2 * CW :])
        more_gh2 = dot_t(gg[...], w[j, :, :CW]) + dot_t(gu[...], w[j, :, CW : 2 * CW])
        branch_ref[...] = more if j == 0 else branch_ref[...] + more
        gh2_ref[...] = more_gh2 if j == 0 else gh2_ref[...] + more_gh2
    for c in outs:
        c.wait()


def back_kernel(
    gain_ref, seg_ref, cos_ref, sin_ref, gt_ref, res_hbm, branch_hbm, gh2_hbm, qkv_hbm, prob_hbm,
    h1_hbm, mixed_hbm, tok_hbm, w_hbm, order_ref,
    out_ref, gin_ref, sib0, sib1, sib2, own0, own1, own2,
    res_ref, branch_ref, gh2_ref, qkv, prob, h1, mixed, tok, wp, wm,
    gr, ga_ref, gm, gp, h1_turned, mixed_turned, gains_turned, tmp, gains_tmp,
    h1t, mt, grads, sems, out_sems,
):
    copies = started(
        [
            (res_hbm, res_ref), (branch_hbm, branch_ref), (gh2_hbm, gh2_ref),
            (w_hbm.at[:, pl.ds(MIX_AT, D)], wm), (qkv_hbm, qkv), (prob_hbm, prob),
            (h1_hbm, h1), (mixed_hbm, mixed),
            (w_hbm.at[:, pl.ds(0, 3 * D)], wp), (tok_hbm, tok),
        ],
        sems,
    )
    for c in copies[:3]:
        c.wait()
    residual = res_ref[...]
    live = seg_ref[...] < 4
    out_ref[...] = jnp.where(live, residual + branch_ref[...], 0.0).astype(bf16)
    xhat2, r2 = norm_parts(residual)
    gh2 = gh2_ref[...]
    second = jnp.sum(gh2 * xhat2, axis=0, keepdims=True)
    n = gh2 * gain_ref[1:2]
    spread = jnp.mean(n * xhat2, axis=-1, keepdims=True)
    grad_res = gt_ref[...].astype(f32) + r2 * (
        n - jnp.mean(n, axis=-1, keepdims=True) - xhat2 * spread
    )
    gr[...] = grad_res
    ga = grad_res.astype(bf16)
    ga_ref[...] = ga
    copies[3].wait()
    gm[...] = dot_t(ga, wm[...]).astype(bf16)
    copies[4].wait()
    copies[5].wait()
    low_half = lax.broadcasted_iota(jnp.int32, (1, PAIR), 1) % HD < HD // 2
    first = lax.broadcasted_iota(jnp.int32, (1, PAIR), 1) < HD
    zero = jnp.zeros((), bf16)

    def pair(p):
        cos, sin = cos_ref[...], sin_ref[...]
        q = qkv[:, pair_slice(p)]
        k = qkv[:, pair_slice(p, D)]
        v = qkv[:, pair_slice(p, 2 * D)]
        g = gm[:, pair_slice(p)]
        dq, dk, dv = [], [], []
        for side in range(2):
            mine = first if side == 0 else jnp.logical_not(first)
            probs = prob[2 * p + side]
            grad_probs = dot_t(jnp.where(mine, g, zero), v)
            weighted = probs * grad_probs
            delta = jnp.sum(weighted, axis=-1, keepdims=True)
            gs = (weighted - probs * delta).astype(bf16)
            dq.append(dot(gs, k))
            dk.append(dot_first(gs, q))
            dv.append(dot_first(probs.astype(bf16), g))
        dq = jnp.where(first, dq[0], dq[1]) * (HD**-0.5)
        dk = jnp.where(first, dk[0], dk[1]) * (HD**-0.5)
        dv = jnp.where(first, dv[0], dv[1])
        gp[:, pair_slice(p)] = (dq * cos - half_swapped(dq, low_half) * sin).astype(bf16)
        gp[:, pair_slice(p, D)] = (dk * cos - half_swapped(dk, low_half) * sin).astype(bf16)
        gp[:, pair_slice(p, 2 * D)] = dv.astype(bf16)

    for p in range(PAIRS):
        pair(p)
    copies[6].wait()
    copies[7].wait()
    h1_turned[...] = jnp.transpose(h1[...].astype(f32))
    mixed_turned[...] = jnp.transpose(mixed[...].astype(f32))
    outs = []
    for j in range(CHUNKS):
        h1t[...] = in_part_order(order_ref, j, h1_turned, tmp)
        mt[...] = in_part_order(order_ref, j, mixed_turned, tmp)
        lo, hi = MIX_CUTS[j]
        to = grads.at[j]
        to[:, pl.ds(0, D)] = dot(h1t[...], gp[:, j * D : (j + 1) * D]).astype(bf16)
        to[:, pl.ds(D, hi - lo)] = dot(mt[...], ga_ref[:, lo:hi]).astype(bf16)
        if j == CHUNKS - 1:
            copies[8].wait()
            copies[9].wait()
            gh1 = dot_t(gp[...], wp[...])
            xhat1, r1 = norm_parts(tok[...].astype(f32))
            one = jnp.sum(gh1 * xhat1, axis=0, keepdims=True)
            m = gh1 * gain_ref[0:1]
            spread = jnp.mean(m * xhat1, axis=-1, keepdims=True)
            gin_ref[...] = gr[...] + r1 * (m - jnp.mean(m, axis=-1, keepdims=True) - xhat1 * spread)
            row = lax.broadcasted_iota(jnp.int32, (128, D), 0)
            both = jnp.where(row == 0, one, jnp.where(row == 1, second, 0.0))
            gains_turned[...] = jnp.transpose(both)
            to[:, pl.ds(D + 256, 128)] = in_part_order(order_ref, j, gains_turned, gains_tmp)
        for half, group in enumerate(((sib0, sib1, sib2), (own0, own1, own2))):
            outs.append(
                pltpu.make_async_copy(
                    grads.at[j, pl.ds(half * ROWS, ROWS)], group[j], out_sems.at[2 * j + half]
                )
            )
            outs[-1].start()
    for c in outs:
        c.wait()


def turn_kernel(ff_terms, *refs):
    send, keep, whole = refs[ff_terms + 4 :]
    at = 0
    for terms in (refs[:ff_terms], refs[ff_terms : ff_terms + 4]):
        total = terms[0][...].astype(f32)
        for t in terms[1:]:
            total = total + t[...].astype(f32)
        whole[:, pl.ds(at, total.shape[1])] = total
        at += total.shape[1]
    send[...] = whole[pl.ds(0, 64), :].astype(bf16)
    keep[...] = whole[pl.ds(64, 64), :].astype(bf16)


def pack_kernel(packed, mixer, expand, reduce, gains, out, wide):
    out[:, pl.ds(0, MIX_AT)] = packed[...]
    out[:, pl.ds(MIX_AT, D)] = mixer[...]
    out[:, pl.ds(GAIN_AT, 128)] = gains[...]
    both = expand[...].astype(f32)
    wide[...] = jnp.zeros(wide.shape, f32)
    wide[0, :, pl.ds(0, FF)] = both[:, :FF]
    wide[1, :, pl.ds(0, FF)] = pltpu.roll(both, FF, 1)[:, :FF]
    wide[2, :, pl.ds(0, FF)] = reduce[...].astype(f32)
    for j in range(CHUNKS):
        for i in range(3):
            out[:, pl.ds(FF_AT + (3 * j + i) * CW, CW)] = wide[i, :, pl.ds(j * CW, CW)].astype(bf16)


def finish_kernel(*refs):
    gots, kepts = refs[:3], refs[3:6]
    packed, mixer, expand, reduce, gain, wide = refs[6:]
    ff = 3 * CW
    for j in range(CHUNKS):
        total = gots[j][...].astype(f32) + kepts[j][...].astype(f32)
        for i in range(3):
            wide[i, :, pl.ds(j * CW, CW)] = total[:, i * CW : (i + 1) * CW]
        packed[:, pl.ds(j * D, D)] = total[:, ff : ff + D]
        lo, hi = MIX_CUTS[j]
        mixer[:, pl.ds(lo, hi - lo)] = total[:, ff + D : ff + D + hi - lo]
    gain[...] = jnp.transpose(total[:, ff + D + 256 :])[:8]
    reduce[...] = wide[2, :, pl.ds(0, FF)]
    lane = lax.broadcasted_iota(jnp.int32, (1, 2 * FF), 1)
    pad = jnp.zeros((8, 2 * FF - CHUNKS * CW), f32)
    gate = jnp.concatenate([wide[0], pad], axis=1)
    up = pltpu.roll(jnp.concatenate([wide[1], pad], axis=1), FF, 1)
    expand[...] = jnp.where(lane < FF, gate, up)


def arr(shape, dtype):
    return jax.ShapeDtypeStruct(shape, dtype)


VSPEC = pl.BlockSpec(memory_space=pltpu.VMEM)
HSPEC = pl.BlockSpec(memory_space=pl.ANY)
SSPEC = pl.BlockSpec(memory_space=pltpu.SMEM)
DMA = pltpu.SemaphoreType.DMA


def run(
    kernel, name, inputs, out_shape, scratch=(), in_hbm=(), out_hbm=(), after=(), through=(), specs=(),
    in_smem=(),
):
    count, outs, extra = len(inputs), len(out_shape), len(after) + len(through)

    def with_order(*refs):
        rest = refs[count + extra :]
        kernel(*refs[:count], *rest[:outs], *rest[outs + len(through) :])

    return pl.pallas_call(
        with_order,
        out_shape=tuple(out_shape) + tuple(arr(t.shape, t.dtype) for t in through),
        grid=(1,) if specs else (),
        in_specs=(
            list(specs)
            or [HSPEC if i in in_hbm else SSPEC if i in in_smem else VSPEC for i in range(count)]
        )
        + [HSPEC] * extra,
        out_specs=tuple(HSPEC if i in out_hbm else VSPEC for i in range(outs))
        + (HSPEC,) * len(through),
        input_output_aliases={count + len(after) + i: outs + i for i in range(len(through))},
        scratch_shapes=list(scratch),
        compiler_params=pltpu.CompilerParams(vmem_limit_bytes=VMEM),
        cost_estimate=pl.CostEstimate(flops=10**14, bytes_accessed=1024, transcendentals=0),
        name=name,
    )(*inputs, *after, *through)


def token_layout(lengths, slot_count):
    places = jnp.arange(slot_count, dtype=jnp.int32)
    ends = jnp.cumsum(lengths)
    starts = ends - lengths
    segment = jnp.sum((places[:, None] >= ends[None, :]).astype(jnp.int32), axis=1)
    live = places < ends[-1]
    picked = (segment[:, None] == jnp.arange(lengths.shape[0], dtype=jnp.int32)[None, :]).astype(
        jnp.int32
    )
    position = jnp.where(live, places - jnp.sum(picked * starts[None, :], axis=1), 0)
    segment = jnp.where(live, segment, lengths.shape[0] + places)
    return segment, position


def rotary_tables(position):
    frequency = rope_base ** (-(jnp.arange(HD // 2, dtype=f32) * 2.0 / HD))
    angles = position.astype(f32)[:, None] * frequency
    cos, sin = jnp.cos(angles), jnp.sin(angles)
    return (
        jnp.concatenate([cos, cos, cos, cos], axis=-1),
        jnp.concatenate([-sin, sin, -sin, sin], axis=-1),
    )


ORDERS = (("x", "y", "z"), ("y", "z", "x"), ("z", "x", "y"))


def hops(core):
    return (1, 3) if core == 0 else (3, 1)


def row_features(order):
    core = lax.axis_index("c")
    row = jnp.arange(D, dtype=jnp.int32)
    mine, inner = row >= ROWS, row % ROWS
    side = jnp.where(mine, core, 1 - core)
    place = {}
    for axis, size in zip(order, (128, 32, 8)):
        turn = inner // size % 4
        apart = jnp.where(turn == 0, 2, jnp.where(turn == 3, 0, jnp.where((turn == 1) == (side == 0), 1, 3)))
        place[axis] = lax.axis_index(axis) ^ apart
    return ((place["y"] * 4 + place["z"]) * 4 + place["x"]) * 16 + side * 8 + inner % 8


def row_order(order):
    return (row_features(order)[:, None] == jnp.arange(D, dtype=jnp.int32)[None, :]).astype(bf16)


def to_partner(a, axis, step):
    pairs = [(i * 2 + c, (i ^ hops(c)[step]) * 2 + c) for i in range(4) for c in range(2)]
    return lax.ppermute(a, (axis, "c"), pairs)


def to_sibling(a):
    return lax.ppermute(a, "c", [(0, 1), (1, 0)])


def added(*arrays):
    total = arrays[0]
    for a in arrays[1:]:
        total = total + a
    return total


class PartSum:
    def __init__(self, order, sib, own):
        self.axis = order[0]
        self.own, self.arrived = own, to_sibling(sib)
        self.lo, self.step, self.got = 0, 0, None

    def piece(self, lo, rows):
        at = slice(lo, lo + rows)
        terms = [self.own[at], self.arrived[at]]
        if self.got is not None:
            terms.append(self.got[lo - self.lo : lo - self.lo + rows])
        return added(*terms)

    def send(self):
        rows = (ROWS - self.lo) // 2
        out = self.piece(self.lo, rows)
        got = to_partner(out, self.axis, self.step)
        self.got = got if self.got is None else (got, self.got)
        self.lo += rows
        self.step += 1
        return out

    def last_terms(self):
        cols = self.own.shape[1]
        got, kept = self.got
        specs = [pl.BlockSpec((128, cols), lambda i, at=at: (at, 0)) for at in (3, 3, 0, 1)]
        return (self.own, self.arrived, got, kept), specs

    def total(self):
        got, kept = self.got
        at = slice(self.lo, ROWS)
        return (added(self.own[at], self.arrived[at], got, kept[ROWS // 4 :]),), [VSPEC]


def halves(a):
    n = a.shape[0] // 2
    return a[:n], a[n:]


def local_step(tokens, cotangent, lengths, weights, perms, part_sum):
    n = tokens.shape[0]
    segment, position = token_layout(lengths, n)
    cos, sin = rotary_tables(position)
    seg_col, seg_row = segment[:, None], segment[None, :]
    tile = arr((n, D), bf16)
    wide = arr((n, D), f32)
    vm = pltpu.VMEM
    orders = jnp.concatenate([row_features(order)[::8] for order in ORDERS])
    gt, *gtts = run(
        cotangent_kernel, "cotangent", (cotangent, seg_col, *perms),
        (tile,) + (arr((D, n), bf16),) * CHUNKS,
    )
    qkv, probs, residual, h1, h2, mixed, gains = run(
        attend_kernel, "attend", (tokens, seg_col, seg_row, cos, sin, weights),
        (arr((n, 3 * D), bf16), arr((H, n, n), f32), wide, tile, tile, tile, arr((8, D), f32)),
        [
            vm((D, 3 * D), bf16), vm((D, D), bf16), vm((D, 128), bf16), vm((n, 3 * D), f32),
            vm((n, n), f32), vm((n, 3 * D), bf16), vm((H, n, n), f32), DMA((3,)), DMA((3,)),
        ],
        in_hbm=(5,),
        out_hbm=(0, 1),
    )
    branch, gh2, *pieces = run(
        gated_kernel, "gated", (orders, h2, gt, *gtts, weights),
        (wide, wide) + (arr((ROWS, 3 * CW), bf16),) * 6,
        [vm((n, D), bf16), vm((n, D), bf16), vm((3, D, n), bf16)]
        + [vm((3, D, 3 * CW), bf16)]
        + [vm((n, CW), f32)] * 3
        + [vm((n, CW), bf16)] * 3
        + [vm((D, n), f32), vm((D, n), f32)]
        + [vm((D, n), bf16), vm((3, D, 3 * CW), bf16), DMA((14,)), DMA((18,))],
        in_hbm=range(1, 7),
        in_smem=(0,),
        out_hbm=range(2, 8),
    )
    ff = [part_sum(ORDERS[j], pieces[j], pieces[3 + j]) for j in range(CHUNKS)]
    after = ()
    for f in ff:
        if after:
            f.own, _ = lax.optimization_barrier((f.own, after[-1]))
        after += (f.send(),)
    block_output, input_grad, *pieces = run(
        back_kernel, "back",
        (gains, seg_col, cos, sin, gt, residual, branch, gh2, qkv, probs, h1, mixed, tokens, weights, orders),
        (tile, wide) + (arr((ROWS, A_COLS), bf16),) * 6,
        [vm((n, D), f32)] * 3
        + [vm((n, 3 * D), bf16), vm((H, n, n), f32)]
        + [vm((n, D), bf16)] * 3
        + [vm((D, 3 * D), bf16), vm((D, D), bf16), vm((n, D), f32), vm((n, D), bf16), vm((n, D), bf16)]
        + [vm((n, 3 * D), bf16), vm((D, n), f32), vm((D, n), f32), vm((D, 128), f32), vm((D, n), f32)]
        + [vm((D, 128), f32), vm((D, n), bf16), vm((D, n), bf16), vm((3, D, A_COLS), bf16)]
        + [DMA((10,)), DMA((6,))],
        in_hbm=range(5, 14),
        in_smem=(14,),
        out_hbm=range(2, 8),
        after=after,
        through=tuple(f.own for f in ff),
    )
    for f, own in zip(ff, pieces[6:]):
        f.own = own
    att = [part_sum(ORDERS[j], pieces[j], pieces[3 + j]) for j in range(CHUNKS)]
    return block_output, input_grad, ff, att


def summed(ff, att):
    for f in ff:
        f.send()
    for f, a in zip(ff, att):
        f.own, _ = lax.optimization_barrier((f.own, a.send()))
    for a in att:
        a.send()
    pairs = []
    for f, a in zip(ff, att):
        f_terms, f_specs = f.total()
        a_terms, a_specs = a.last_terms()
        cols = f.own.shape[1] + a.own.shape[1]
        pairs.append(
            run(
                functools.partial(turn_kernel, len(f_terms)), "turn", f_terms + a_terms, (arr((64, cols), bf16),) * 2,
                [pltpu.VMEM((128, cols), f32)], specs=f_specs + a_specs,
            )
        )
    for ring, step in ((1, 0), (1, 1), (2, 0), (2, 1)):
        gots = [to_partner(p[0], order[ring], step) for p, order in zip(pairs, ORDERS)]
        kept = [p[1] for p in pairs]
        if (ring, step) != (2, 1):
            pairs = [halves(added(g, k)) for g, k in zip(gots, kept)]
    return gots, kept


def own_rows(gots, kept):
    n = 8
    *grads, gains = run(
        finish_kernel, "finish", (*gots, *kept),
        tuple(arr((n, c), f32) for c in (3 * D, D, 2 * FF, FF, 8)),
        [pltpu.VMEM((3, n, CHUNKS * CW), f32)],
    )
    return (*grads, gains[0], gains[1])


def body(
    tokens, packed_proj, mixer_proj, expand_proj, reduce_proj, first_gain, second_gain,
    sequence_lengths, cotangent,
):
    gains = jnp.pad(jnp.stack([first_gain, second_gain], axis=1), ((0, 0), (0, 126)))
    (shard,) = run(
        pack_kernel, "pack", (packed_proj, mixer_proj, expand_proj, reduce_proj, gains),
        (arr((8, W_COLS), bf16),), [pltpu.VMEM((3, 8, CHUNKS * CW), f32)],
    )
    weights = lax.all_gather(shard, ALL, axis=0, tiled=True)
    perms = [row_order(order) for order in ORDERS]
    block_output, input_grad, ff, att = local_step(
        tokens, cotangent, sequence_lengths, weights, perms, PartSum
    )
    return (block_output, input_grad, *own_rows(*summed(ff, att)))


def solution(mesh):
    torus = Mesh(mesh.devices.reshape(4, 4, 4, 2), ALL)
    row, flat = P(ALL, None), P(ALL)
    return jax.shard_map(
        body,
        mesh=torus,
        in_specs=(row,) * 5 + (flat, flat, flat, row),
        out_specs=(row,) * 6 + (flat, flat),
        check_vma=False,
    )
```

profile of v0, /device:TPU:0, one launch (start us, length us, event | category | flops | bytes accessed | tf_op | source)
XLA Modules:
  0.0 278.3 jit_solution(13514450361514348155)
XLA Ops:
  7.2 0.7 pad_maximum_fusion.2
  8.6 1.7 pack.1
  11.5 1.7 fusion.refs_2_
  13.2 1.8 fusion.1.refs_3_
  15.0 1.7 fusion.2.refs_4_
  16.7 1.3 add_select_fusion.refs_1_
  18.1 6.0 %cotangent.1 = (bf16[256,1024]{1,0:T(8,128)(2,1)}, bf16[1024,256]{1,0:T(8,128)(2,1)}, bf16[1024,256]{1,0:T(8,128)(2,1)}, bf16[1024,256]{1,0:T(8,128)(2,1)}) custom-call(bf16[256,1024]{1,0:T(8,128)(2,1)} %refs_0_.5, s32[256,1]{1,0:T(8,128)} %add_select_fusion.refs_1_, bf16[1024,1024]{1,0:T(8,128)(2,1)} %fusion.refs_2_, bf16[1024,1024]{1,0:T(8,128)(2,1)} %fusion.1.refs_3_, ...), custom_call_target="tpu_custom_call" | custom-call | flops 100000000376832 | bytes 1024 | tf_op jit(solution)/shard_map/cotangent/pallas_call | solution.py:381
  24.1 0.9 slice.191
  25.0 0.9 slice.192
  25.9 0.9 slice.193
  27.5 0.6 fusion.25
  28.7 1.0 pad_maximum_fusion
  29.7 1.2 compare_select_fusion.refs_2_
  30.9 76.4 %all-gather.2.cloned.1.call-done.refs_5_.refs_6_.refs_13_ = bf16[1024,12288]{1,0:T(8,128)(2,1)} async-done(((bf16[8,12288]{1,0:T(8,128)(2,1)}), bf16[1024,12288]{1,0:T(8,128)(2,1)}) %all-gather.2.cloned.1.call-update) | async-done | bytes 25165840 | tf_op jit(solution)/shard_map/all_gather | solution.py:613
  107.3 11.0 %attend.1 = (bf16[256,3072]{1,0:T(8,128)(2,1)}, f32[16,256,256]{2,1,0:T(8,128)}, f32[256,1024]{1,0:T(8,128)}, bf16[256,1024]{1,0:T(8,128)(2,1)}, bf16[256,1024]{...) custom-call(bf16[256,1024]{1,0:T(8,128)(2,1)} %refs_12_.1, s32[256,1]{1,0:T(8,128)} %add_select_fusion.refs_1_, ...), custom_call_target="tpu_custom_call" | custom-call | flops 100000000376832 | bytes 1024 | tf_op jit(solution)/shard_map/attend/pallas_call | solution.py:381
  118.3 23.2 %gated.1 = (f32[256,1024]{1,0:T(8,128)}, f32[256,1024]{1,0:T(8,128)}, bf16[512,2688]{1,0:T(8,128)(2,1)}, bf16[512,2688]{1,0:T(8,128)(2,1)}, bf16[512,2688]{1,0:T...) custom-call(s32[384]{0:T(512)} %pad_add_fusion.refs_0_.refs_14_, ...), custom_call_target="tpu_custom_call" | custom-call | flops 100000000376832 | bytes 1024 | tf_op jit(solution)/shard_map/gated/pallas_call | solution.py:381
  142.4 4.5 %collective-permute-done = bf16[512,2688]{1,0:T(8,128)(2,1)S(1)} collective-permute-done((bf16[512,2688]{1,0:T(8,128)(2,1)}, bf16[512,2688]{1,0:T(8,128)(2,1)S(1)}, u32[]{:S(2)}, u32[]{:S(2)}) %collective-permute-start) | collective-permute-done | bytes 2752544 | tf_op jit(solution)/shard_map/ppermute | solution.py:454
  146.9 3.7 %slice_add_fusion.2.refs_15_ = bf16[256,2688]{1,0:T(8,128)(2,1)} fusion(bf16[512,2688]{1,0:T(8,128)(2,1)S(1)} %collective-permute-done, bf16[512,2688]{1,0:T(8,128)(2,1)} %get-tuple-element.67.refs_18_), kind=kLoop, calls=%fused_computation.8 | loop fusion | flops 688128 | bytes 4128768 | tf_op jit(solution)/shard_map/add | solution.py:460
  150.6 1.5 collective-permute-start.4
  152.0 1.4 slice_add_fusion.1.refs_16_
  153.4 1.5 collective-permute-start.13
  154.9 1.4 slice_add_fusion.refs_17_
  156.3 9.3 %collective-permute-start.22 = (bf16[256,2688]{1,0:T(8,128)(2,1)}, bf16[256,2688]{1,0:T(8,128)(2,1)}, u32[]{:S(2)}, u32[]{:S(2)}) collective-permute-start(bf16[256,2688]{1,0:T(8,128)(2,1)} %slice_add_fusion.refs_17_), channel_id=1, source_target_pairs={{0,8},{1,25},{8,0},{9,17},{16,24},{17,9},{24,16},{25,1},{2,10},{3,... | collective-permute-start | bytes 4128776 | tf_op jit(solution)/shard_map/ppermute | solution.py:450
  165.6 20.0 %back.1 = (bf16[256,1024]{1,0:T(8,128)(2,1)}, f32[256,1024]{1,0:T(8,128)}, bf16[512,1408]{1,0:T(8,128)(2,1)}, bf16[512,1408]{1,0:T(8,128)(2,1)}, bf16[512,1408]{...) custom-call(f32[8,1024]{1,0:T(8,128)} %get-tuple-element.54.refs_0_,, ...), custom_call_target="tpu_custom_call", output_to_operand_aliasing={{8}: (18, {}), {9}: (19, {}), {10}: (20, {})} | custom-call | flops 100000000376832 | bytes 1024 | tf_op jit(solution)/shard_map/back/pallas_call | solution.py:381
  185.6 1.9 collective-permute-start.21
  188.3 1.4 slice_add_fusion.7
  189.7 2.5 collective-permute-start.23
  192.3 1.6 slice_add_fusion.11
  193.8 0.8 collective-permute-start.14
  194.6 1.4 slice_add_fusion.15
  196.1 2.8 collective-permute-start.5
  199.6 5.3 %collective-permute-done.23 = bf16[128,2688]{1,0:T(8,128)(2,1)S(1)} collective-permute-done((bf16[128,2688]{1,0:T(8,128)(2,1)S(1)}, bf16[128,2688]{1,0:T(8,128)(2,1)S(1)}, u32[]{:S(2)}, u32[]{:S(2)}) %collective-permute-start.23) | collective-permute-done | bytes 688160 | tf_op jit(solution)/shard_map/ppermute | solution.py:450
  205.5 2.4 slice_add_fusion.6.refs_0_
  207.9 4.1 %collective-permute-done.14 = bf16[128,2688]{1,0:T(8,128)(2,1)S(1)} collective-permute-done((bf16[128,2688]{1,0:T(8,128)(2,1)S(1)}, bf16[128,2688]{1,0:T(8,128)(2,1)S(1)}, u32[]{:S(2)}, u32[]{:S(2)}) %collective-permute-start.14) | collective-permute-done | bytes 688160 | tf_op jit(solution)/shard_map/ppermute | solution.py:450
  212.0 2.3 slice_add_fusion.10.refs_0_
  214.3 2.3 slice_add_fusion.14.refs_0_
  216.7 0.8 collective-permute-start.25
  217.5 0.9 slice_add_fusion.20
  218.4 1.4 collective-permute-start.16
  219.8 0.9 slice_add_fusion.22
  220.8 1.4 collective-permute-start.7
  222.2 3.3 %collective-permute-done.25.refs_3_ = bf16[128,1408]{1,0:T(8,128)(2,1)S(1)} collective-permute-done((bf16[128,1408]{1,0:T(8,128)(2,1)S(1)}, bf16[128,1408]{1,0:T(8,128)(2,1)S(1)}, u32[]{:S(2)}, u32[]{:S(2)}) %collective-permute-start.25) | collective-permute-done | bytes 360480 | tf_op jit(solution)/shard_map/ppermute | solution.py:450
  225.4 0.7 copy-done.25
  226.2 2.6 turn.5
  228.8 2.6 turn.4
  231.4 2.3 collective-permute-done.7.refs_3_
  233.6 2.7 turn.3
  236.4 2.2 collective-permute-done.26
  238.5 1.2 add.477
  239.7 1.6 collective-permute-start.27
  241.3 1.1 collective-permute-done.17
  242.4 1.2 add.466
  243.7 4.9 %collective-permute-done.8 = bf16[64,4096]{1,0:T(8,128)(2,1)S(1)} collective-permute-done((bf16[64,4096]{1,0:T(8,128)(2,1)}, bf16[64,4096]{1,0:T(8,128)(2,1)S(1)}, u32[]{:S(2)}, u32[]{:S(2)}) %collective-permute-start.8) | collective-permute-done | bytes 524320 | tf_op jit(solution)/shard_map/ppermute | solution.py:450
  248.7 1.9 collective-permute-start.9
  250.7 1.3 collective-permute-done.18
  252.1 3.0 %collective-permute-start.19 = (bf16[16,4096]{1,0:T(8,128)(2,1)S(1)}, bf16[16,4096]{1,0:T(8,128)(2,1)S(1)}, u32[]{:S(2)}, u32[]{:S(2)}) collective-permute-start(bf16[16,4096]{1,0:T(8,128)(2,1)S(1)} %slice.277), channel_id=1, source_target_pairs={{0,2},{1,7},{2,0},{3,5},{4,6},{5,3},{6,4},{7,1},{8,10},{9,15},{10,... | collective-permute-start | bytes 393224 | tf_op jit(solution)/shard_map/ppermute | solution.py:450
  255.1 1.3 collective-permute-done.9
  256.5 0.6 fusion.26
  257.2 1.8 collective-permute-start.29
  259.6 1.6 collective-permute-start.20
  262.1 2.5 collective-permute-start.11
  265.1 2.5 collective-permute-done.11.refs_0_
  268.2 1.8 finish.1
  270.0 1.3 slice_bitcast_fusion
  (132 shorter events, 9.4 us)
Async XLA Ops:
  7.2 100.1 %all-gather.2.cloned.1.call-start = ((), (), s32[]{:S(2)}) async-start(), calls=%async_computation | async-start | bytes 25362432 | tf_op jit(solution)/shard_map/all_gather | solution.py:613
  8.6 1.9 copy-start.29
  10.4 4.6 %copy-start.20 = (s32[1024]{0:T(1024)}, s32[1024]{0:T(1024)S(1)}, u32[]{:S(2)}) copy-start(s32[1024]{0:T(1024)S(1)} %get-tuple-element.114) | copy-start | bytes 12292
  10.4 4.6 %copy-start.21 = (s32[1024]{0:T(1024)}, s32[1024]{0:T(1024)S(1)}, u32[]{:S(2)}) copy-start(s32[1024]{0:T(1024)S(1)} %get-tuple-element.113) | copy-start | bytes 12292
  10.5 4.6 %copy-start.22 = (s32[1024]{0:T(1024)}, s32[1024]{0:T(1024)S(1)}, u32[]{:S(2)}) copy-start(s32[1024]{0:T(1024)S(1)} %fusion.12) | copy-start | bytes 12292
  10.7 0.7 copy-start.31
  11.3 3.7 %copy-start.23 = (s32[256]{0:T(256)}, s32[256]{0:T(256)S(1)}, u32[]{:S(2)}) copy-start(s32[256]{0:T(256)S(1)} %convert_reduce_fusion) | copy-start | bytes 3076
  18.1 9.3 %copy-start.30 = (s32[4]{0:T(128)S(1)}, s32[4]{0:T(128)}, u32[]{:S(2)}) copy-start(s32[4]{0:T(128)} %param.16) | copy-start | bytes 52
  18.1 9.3 %copy-start.32 = (s32[4,1]{0,1:T(1,128)S(1)}, s32[4,1]{0,1:T(1,128)}, u32[]{:S(2)}) copy-start(s32[4,1]{0,1:T(1,128)} %copy-done.31) | copy-start | bytes 52
  18.1 9.3 %copy-start.24 = (s32[256]{0:T(256)S(1)}, s32[256]{0:T(256)}, u32[]{:S(2)}) copy-start(s32[256]{0:T(256)} %copy-done.23) | copy-start | bytes 3076
  141.5 10.5 %copy-start.6 = (bf16[512,2688]{1,0:T(8,128)(2,1)S(1)}, bf16[512,2688]{1,0:T(8,128)(2,1)}, u32[]{:S(2)}) copy-start(bf16[512,2688]{1,0:T(8,128)(2,1)} %get-tuple-element.70.refs_19_) | copy-start | bytes 8257540
  141.5 5.4 %collective-permute-start = (bf16[512,2688]{1,0:T(8,128)(2,1)}, bf16[512,2688]{1,0:T(8,128)(2,1)S(1)}, u32[]{:S(2)}, u32[]{:S(2)}) collective-permute-start(bf16[512,2688]{1,0:T(8,128)(2,1)} %get-tuple-element.68), channel_id=1, source_target_pairs={{0,1},{1,0},{2,3},{3,2},{4,5},{5,4},{6,7},{7,6},{8,9},{9,8},{10,11... | collective-permute-start | bytes 8257544 | tf_op jit(solution)/shard_map/ppermute | solution.py:454
  141.9 10.2 %collective-permute-start.1 = (bf16[512,2688]{1,0:T(8,128)(2,1)}, bf16[512,2688]{1,0:T(8,128)(2,1)S(1)}, u32[]{:S(2)}, u32[]{:S(2)}) collective-permute-start(bf16[512,2688]{1,0:T(8,128)(2,1)} %get-tuple-element.71), channel_id=1, source_target_pairs={{0,1},{1,0},{2,3},{3,2},{4,5},{5,4},{6,7},{7,6},{8,9},{9,8},{10,11... | collective-permute-start | bytes 8257544 | tf_op jit(solution)/shard_map/ppermute | solution.py:454
  142.1 12.8 %collective-permute-start.2 = (bf16[512,2688]{1,0:T(8,128)(2,1)}, bf16[512,2688]{1,0:T(8,128)(2,1)S(1)}, u32[]{:S(2)}, u32[]{:S(2)}) collective-permute-start(bf16[512,2688]{1,0:T(8,128)(2,1)} %get-tuple-element.74), channel_id=1, source_target_pairs={{0,1},{1,0},{2,3},{3,2},{4,5},{5,4},{6,7},{7,6},{8,9},{9,8},{10,11... | collective-permute-start | bytes 8257544 | tf_op jit(solution)/shard_map/ppermute | solution.py:454
  146.9 6.5 %copy-start = (bf16[512,2688]{1,0:T(8,128)(2,1)}, bf16[512,2688]{1,0:T(8,128)(2,1)S(1)}, u32[]{:S(2)}) copy-start(bf16[512,2688]{1,0:T(8,128)(2,1)S(1)} %collective-permute-done) | copy-start | bytes 8257540
  150.6 4.3 %copy-start.7 = (bf16[512,2688]{1,0:T(8,128)(2,1)S(1)}, bf16[512,2688]{1,0:T(8,128)(2,1)}, u32[]{:S(2)}) copy-start(bf16[512,2688]{1,0:T(8,128)(2,1)} %get-tuple-element.73.refs_20_) | copy-start | bytes 8257540
  150.6 43.3 %collective-permute-start.4 = (bf16[256,2688]{1,0:T(8,128)(2,1)}, bf16[256,2688]{1,0:T(8,128)(2,1)}, u32[]{:S(2)}, u32[]{:S(2)}) collective-permute-start(bf16[256,2688]{1,0:T(8,128)(2,1)} %slice_add_fusion.2.refs_15_), channel_id=1, source_target_pairs={{0,2},{1,7},{2,0},{3,5},{4,6},{5,3},{6,4},{7,1},{8,10},{9,15},{10,... | collective-permute-start | bytes 4128776 | tf_op jit(solution)/shard_map/ppermute | solution.py:450
  152.0 4.2 %copy-start.2 = (bf16[512,2688]{1,0:T(8,128)(2,1)}, bf16[512,2688]{1,0:T(8,128)(2,1)S(1)}, u32[]{:S(2)}) copy-start(bf16[512,2688]{1,0:T(8,128)(2,1)S(1)} %collective-permute-done.1) | copy-start | bytes 8257540
  153.4 36.3 %collective-permute-start.13 = (bf16[256,2688]{1,0:T(8,128)(2,1)}, bf16[256,2688]{1,0:T(8,128)(2,1)}, u32[]{:S(2)}, u32[]{:S(2)}) collective-permute-start(bf16[256,2688]{1,0:T(8,128)(2,1)} %slice_add_fusion.1.refs_16_), channel_id=1, source_target_pairs={{0,32},{1,97},{32,0},{33,65},{64,96},{65,33},{96,64},{97,1},{2,34}... | collective-permute-start | bytes 4128776 | tf_op jit(solution)/shard_map/ppermute | solution.py:450
  154.9 10.7 %copy-start.4 = (bf16[512,2688]{1,0:T(8,128)(2,1)}, bf16[512,2688]{1,0:T(8,128)(2,1)S(1)}, u32[]{:S(2)}) copy-start(bf16[512,2688]{1,0:T(8,128)(2,1)S(1)} %collective-permute-done.2) | copy-start | bytes 8257540
  156.3 31.6 %collective-permute-start.22 = (bf16[256,2688]{1,0:T(8,128)(2,1)}, bf16[256,2688]{1,0:T(8,128)(2,1)}, u32[]{:S(2)}, u32[]{:S(2)}) collective-permute-start(bf16[256,2688]{1,0:T(8,128)(2,1)} %slice_add_fusion.refs_17_), channel_id=1, source_target_pairs={{0,8},{1,25},{8,0},{9,17},{16,24},{17,9},{24,16},{25,1},{2,10},{3,... | collective-permute-start | bytes 4128776 | tf_op jit(solution)/shard_map/ppermute | solution.py:450
  165.6 22.7 %copy-start.5 = (bf16[512,2688]{1,0:T(8,128)(2,1)S(1)}, bf16[512,2688]{1,0:T(8,128)(2,1)}, u32[]{:S(2)}) copy-start(bf16[512,2688]{1,0:T(8,128)(2,1)} %copy-done.4) | copy-start | bytes 8257540
  185.6 6.6 %copy-start.3 = (bf16[512,2688]{1,0:T(8,128)(2,1)S(1)}, bf16[512,2688]{1,0:T(8,128)(2,1)}, u32[]{:S(2)}) copy-start(bf16[512,2688]{1,0:T(8,128)(2,1)} %copy-done.2) | copy-start | bytes 8257540
  185.6 10.5 %collective-permute-start.21 = (bf16[512,1408]{1,0:T(8,128)(2,1)}, bf16[512,1408]{1,0:T(8,128)(2,1)S(1)}, u32[]{:S(2)}, u32[]{:S(2)}) collective-permute-start(bf16[512,1408]{1,0:T(8,128)(2,1)} %get-tuple-element.91), channel_id=1, source_target_pairs={{0,1},{1,0},{2,3},{3,2},{4,5},{5,4},{6,7},{7,6},{8,9},{9,8},{10,11... | collective-permute-start | bytes 4325384 | tf_op jit(solution)/shard_map/ppermute | solution.py:454
  187.6 11.4 %collective-permute-start.12 = (bf16[512,1408]{1,0:T(8,128)(2,1)}, bf16[512,1408]{1,0:T(8,128)(2,1)S(1)}, u32[]{:S(2)}, u32[]{:S(2)}) collective-permute-start(bf16[512,1408]{1,0:T(8,128)(2,1)} %get-tuple-element.85), channel_id=1, source_target_pairs={{0,1},{1,0},{2,3},{3,2},{4,5},{5,4},{6,7},{7,6},{8,9},{9,8},{10,11... | collective-permute-start | bytes 4325384 | tf_op jit(solution)/shard_map/ppermute | solution.py:454
  187.9 11.3 %collective-permute-start.3 = (bf16[512,1408]{1,0:T(8,128)(2,1)}, bf16[512,1408]{1,0:T(8,128)(2,1)S(1)}, u32[]{:S(2)}, u32[]{:S(2)}) collective-permute-start(bf16[512,1408]{1,0:T(8,128)(2,1)} %get-tuple-element.79), channel_id=1, source_target_pairs={{0,1},{1,0},{2,3},{3,2},{4,5},{5,4},{6,7},{7,6},{8,9},{9,8},{10,11... | collective-permute-start | bytes 4325384 | tf_op jit(solution)/shard_map/ppermute | solution.py:454
  189.7 4.9 %copy-start.1 = (bf16[512,2688]{1,0:T(8,128)(2,1)S(1)}, bf16[512,2688]{1,0:T(8,128)(2,1)}, u32[]{:S(2)}) copy-start(bf16[512,2688]{1,0:T(8,128)(2,1)} %copy-done) | copy-start | bytes 8257540
  189.7 15.2 %collective-permute-start.23 = (bf16[128,2688]{1,0:T(8,128)(2,1)S(1)}, bf16[128,2688]{1,0:T(8,128)(2,1)S(1)}, u32[]{:S(2)}, u32[]{:S(2)}) collective-permute-start(bf16[128,2688]{1,0:T(8,128)(2,1)S(1)} %slice_add_fusion.7), channel_id=1, source_target_pairs={{0,24},{1,9},{8,16},{9,1},{16,8},{17,25},{24,0},{25,17},{2,26},{3,... | collective-permute-start | bytes 2064392 | tf_op jit(solution)/shard_map/ppermute | solution.py:450
  192.3 6.6 %copy-start.10 = (bf16[512,1408]{1,0:T(8,128)(2,1)S(1)}, bf16[512,1408]{1,0:T(8,128)(2,1)}, u32[]{:S(2)}) copy-start(bf16[512,1408]{1,0:T(8,128)(2,1)} %get-tuple-element.90.refs_1_) | copy-start | bytes 4325380
  193.8 5.3 %copy-start.9 = (bf16[512,1408]{1,0:T(8,128)(2,1)S(1)}, bf16[512,1408]{1,0:T(8,128)(2,1)}, u32[]{:S(2)}) copy-start(bf16[512,1408]{1,0:T(8,128)(2,1)} %get-tuple-element.84.refs_1_) | copy-start | bytes 4325380
  193.8 18.1 %collective-permute-start.14 = (bf16[128,2688]{1,0:T(8,128)(2,1)S(1)}, bf16[128,2688]{1,0:T(8,128)(2,1)S(1)}, u32[]{:S(2)}, u32[]{:S(2)}) collective-permute-start(bf16[128,2688]{1,0:T(8,128)(2,1)S(1)} %slice_add_fusion.11), channel_id=1, source_target_pairs={{0,96},{1,33},{32,64},{33,1},{64,32},{65,97},{96,0},{97,65},{2,98}... | collective-permute-start | bytes 2064392 | tf_op jit(solution)/shard_map/ppermute | solution.py:450
  196.1 3.4 %copy-start.8 = (bf16[512,1408]{1,0:T(8,128)(2,1)S(1)}, bf16[512,1408]{1,0:T(8,128)(2,1)}, u32[]{:S(2)}) copy-start(bf16[512,1408]{1,0:T(8,128)(2,1)} %get-tuple-element.78.refs_1_) | copy-start | bytes 4325380
  196.1 20.5 %copy-start.13 = (bf16[512,1408]{1,0:T(8,128)(2,1)}, bf16[512,1408]{1,0:T(8,128)(2,1)S(1)}, u32[]{:S(2)}) copy-start(bf16[512,1408]{1,0:T(8,128)(2,1)S(1)} %collective-permute-done.21.refs_2_) | copy-start | bytes 4325380
  196.1 18.2 %collective-permute-start.5 = (bf16[128,2688]{1,0:T(8,128)(2,1)S(1)}, bf16[128,2688]{1,0:T(8,128)(2,1)S(1)}, u32[]{:S(2)}, u32[]{:S(2)}) collective-permute-start(bf16[128,2688]{1,0:T(8,128)(2,1)S(1)} %slice_add_fusion.15), channel_id=1, source_target_pairs={{0,6},{1,3},{2,4},{3,1},{4,2},{5,7},{6,0},{7,5},{8,14},{9,11},{10,... | collective-permute-start | bytes 2064392 | tf_op jit(solution)/shard_map/ppermute | solution.py:450
  199.0 18.5 %copy-start.12 = (bf16[512,1408]{1,0:T(8,128)(2,1)}, bf16[512,1408]{1,0:T(8,128)(2,1)S(1)}, u32[]{:S(2)}) copy-start(bf16[512,1408]{1,0:T(8,128)(2,1)S(1)} %collective-permute-done.12.refs_2_) | copy-start | bytes 4325380
  199.0 17.7 %collective-permute-start.24 = (bf16[256,1408]{1,0:T(8,128)(2,1)S(1)}, bf16[256,1408]{1,0:T(8,128)(2,1)S(1)}, u32[]{:S(2)}, u32[]{:S(2)}) collective-permute-start(bf16[256,1408]{1,0:T(8,128)(2,1)S(1)} %slice_add_fusion.3), channel_id=1, source_target_pairs={{0,8},{1,25},{8,0},{9,17},{16,24},{17,9},{24,16},{25,1},{2,10},{3,... | collective-permute-start | bytes 2162696 | tf_op jit(solution)/shard_map/ppermute | solution.py:450
  199.2 20.6 %copy-start.11 = (bf16[512,1408]{1,0:T(8,128)(2,1)}, bf16[512,1408]{1,0:T(8,128)(2,1)S(1)}, u32[]{:S(2)}) copy-start(bf16[512,1408]{1,0:T(8,128)(2,1)S(1)} %collective-permute-done.3.refs_2_) | copy-start | bytes 4325380
  199.2 18.3 %collective-permute-start.15 = (bf16[256,1408]{1,0:T(8,128)(2,1)S(1)}, bf16[256,1408]{1,0:T(8,128)(2,1)S(1)}, u32[]{:S(2)}, u32[]{:S(2)}) collective-permute-start(bf16[256,1408]{1,0:T(8,128)(2,1)S(1)} %slice_add_fusion.4), channel_id=1, source_target_pairs={{0,32},{1,97},{32,0},{33,65},{64,96},{65,33},{96,64},{97,1},{2,34}... | collective-permute-start | bytes 2162696 | tf_op jit(solution)/shard_map/ppermute | solution.py:450
  204.9 14.8 %collective-permute-start.6 = (bf16[256,1408]{1,0:T(8,128)(2,1)S(1)}, bf16[256,1408]{1,0:T(8,128)(2,1)S(1)}, u32[]{:S(2)}, u32[]{:S(2)}) collective-permute-start(bf16[256,1408]{1,0:T(8,128)(2,1)S(1)} %slice_add_fusion.5), channel_id=1, source_target_pairs={{0,2},{1,7},{2,0},{3,5},{4,6},{5,3},{6,4},{7,1},{8,10},{9,15},{10,... | collective-permute-start | bytes 2162696 | tf_op jit(solution)/shard_map/ppermute | solution.py:450
  216.6 4.0 %copy-start.19 = (bf16[256,1408]{1,0:T(8,128)(2,1)}, bf16[256,1408]{1,0:T(8,128)(2,1)S(1)}, u32[]{:S(2)}) copy-start(bf16[256,1408]{1,0:T(8,128)(2,1)S(1)} %collective-permute-done.24.refs_4_) | copy-start | bytes 2162692
  216.7 8.7 %collective-permute-start.25 = (bf16[128,1408]{1,0:T(8,128)(2,1)S(1)}, bf16[128,1408]{1,0:T(8,128)(2,1)S(1)}, u32[]{:S(2)}, u32[]{:S(2)}) collective-permute-start(bf16[128,1408]{1,0:T(8,128)(2,1)S(1)} %slice_add_fusion.18), channel_id=1, source_target_pairs={{0,24},{1,9},{8,16},{9,1},{16,8},{17,25},{24,0},{25,17},{2,26},{3,... | collective-permute-start | bytes 1081352 | tf_op jit(solution)/shard_map/ppermute | solution.py:450
  217.5 4.7 %copy-start.18 = (bf16[256,1408]{1,0:T(8,128)(2,1)}, bf16[256,1408]{1,0:T(8,128)(2,1)S(1)}, u32[]{:S(2)}) copy-start(bf16[256,1408]{1,0:T(8,128)(2,1)S(1)} %collective-permute-done.15.refs_4_) | copy-start | bytes 2162692
  218.4 10.4 %collective-permute-start.16 = (bf16[128,1408]{1,0:T(8,128)(2,1)}, bf16[128,1408]{1,0:T(8,128)(2,1)}, u32[]{:S(2)}, u32[]{:S(2)}) collective-permute-start(bf16[128,1408]{1,0:T(8,128)(2,1)} %slice_add_fusion.20), channel_id=1, source_target_pairs={{0,96},{1,33},{32,64},{33,1},{64,32},{65,97},{96,0},{97,65},{2,98}... | collective-permute-start | bytes 1081352 | tf_op jit(solution)/shard_map/ppermute | solution.py:450
  219.8 1.1 copy-start.17
  220.8 12.8 %collective-permute-start.7 = (bf16[128,1408]{1,0:T(8,128)(2,1)}, bf16[128,1408]{1,0:T(8,128)(2,1)}, u32[]{:S(2)}, u32[]{:S(2)}) collective-permute-start(bf16[128,1408]{1,0:T(8,128)(2,1)} %slice_add_fusion.22), channel_id=1, source_target_pairs={{0,6},{1,3},{2,4},{3,1},{4,2},{5,7},{6,0},{7,5},{8,14},{9,11},{10,... | collective-permute-start | bytes 1081352 | tf_op jit(solution)/shard_map/ppermute | solution.py:450
  225.4 0.7 copy-start.25
  228.8 9.7 %collective-permute-start.26 = (bf16[64,4096]{1,0:T(8,128)(2,1)}, bf16[64,4096]{1,0:T(8,128)(2,1)}, u32[]{:S(2)}, u32[]{:S(2)}) collective-permute-start(bf16[64,4096]{1,0:T(8,128)(2,1)} %get-tuple-element.93), channel_id=1, source_target_pairs={{0,2},{1,7},{2,0},{3,5},{4,6},{5,3},{6,4},{7,1},{8,10},{9,15},{10,... | collective-permute-start | bytes 1572872 | tf_op jit(solution)/shard_map/ppermute | solution.py:450
  231.4 11.0 %collective-permute-start.17 = (bf16[64,4096]{1,0:T(8,128)(2,1)}, bf16[64,4096]{1,0:T(8,128)(2,1)}, u32[]{:S(2)}, u32[]{:S(2)}) collective-permute-start(bf16[64,4096]{1,0:T(8,128)(2,1)} %get-tuple-element.87), channel_id=1, source_target_pairs={{0,8},{1,25},{8,0},{9,17},{16,24},{17,9},{24,16},{25,1},{2,10},{3,... | collective-permute-start | bytes 1572872 | tf_op jit(solution)/shard_map/ppermute | solution.py:450
  233.6 4.9 %copy-start.14 = (bf16[64,4096]{1,0:T(8,128)(2,1)S(1)}, bf16[64,4096]{1,0:T(8,128)(2,1)}, u32[]{:S(2)}) copy-start(bf16[64,4096]{1,0:T(8,128)(2,1)} %get-tuple-element.94) | copy-start | bytes 1572868
  236.3 6.0 %copy-start.15 = (bf16[64,4096]{1,0:T(8,128)(2,1)S(1)}, bf16[64,4096]{1,0:T(8,128)(2,1)}, u32[]{:S(2)}) copy-start(bf16[64,4096]{1,0:T(8,128)(2,1)} %get-tuple-element.88) | copy-start | bytes 1572868
  236.3 12.2 %copy-start.16 = (bf16[64,4096]{1,0:T(8,128)(2,1)S(1)}, bf16[64,4096]{1,0:T(8,128)(2,1)}, u32[]{:S(2)}) copy-start(bf16[64,4096]{1,0:T(8,128)(2,1)} %get-tuple-element.82) | copy-start | bytes 1572868
  236.3 12.2 %collective-permute-start.8 = (bf16[64,4096]{1,0:T(8,128)(2,1)}, bf16[64,4096]{1,0:T(8,128)(2,1)S(1)}, u32[]{:S(2)}, u32[]{:S(2)}) collective-permute-start(bf16[64,4096]{1,0:T(8,128)(2,1)} %get-tuple-element.81), channel_id=1, source_target_pairs={{0,32},{1,97},{32,0},{33,65},{64,96},{65,33},{96,64},{97,1},{2,34}... | collective-permute-start | bytes 1572872 | tf_op jit(solution)/shard_map/ppermute | solution.py:450
  239.7 10.9 %collective-permute-start.27 = (bf16[32,4096]{1,0:T(8,128)(2,1)S(1)}, bf16[32,4096]{1,0:T(8,128)(2,1)S(1)}, u32[]{:S(2)}, u32[]{:S(2)}) collective-permute-start(bf16[32,4096]{1,0:T(8,128)(2,1)S(1)} %slice.287), channel_id=1, source_target_pairs={{0,6},{1,3},{2,4},{3,1},{4,2},{5,7},{6,0},{7,5},{8,14},{9,11},{10,... | collective-permute-start | bytes 786440 | tf_op jit(solution)/shard_map/ppermute | solution.py:450
  243.6 8.5 %collective-permute-start.18 = (bf16[32,4096]{1,0:T(8,128)(2,1)S(1)}, bf16[32,4096]{1,0:T(8,128)(2,1)S(1)}, u32[]{:S(2)}, u32[]{:S(2)}) collective-permute-start(bf16[32,4096]{1,0:T(8,128)(2,1)S(1)} %slice.275), channel_id=1, source_target_pairs={{0,24},{1,9},{8,16},{9,1},{16,8},{17,25},{24,0},{25,17},{2,26},{3,... | collective-permute-start | bytes 786440 | tf_op jit(solution)/shard_map/ppermute | solution.py:450
  248.7 7.7 %collective-permute-start.9 = (bf16[32,4096]{1,0:T(8,128)(2,1)S(1)}, bf16[32,4096]{1,0:T(8,128)(2,1)S(1)}, u32[]{:S(2)}, u32[]{:S(2)}) collective-permute-start(bf16[32,4096]{1,0:T(8,128)(2,1)S(1)} %slice.263), channel_id=1, source_target_pairs={{0,96},{1,33},{32,64},{33,1},{64,32},{65,97},{96,0},{97,65},{2,98}... | collective-permute-start | bytes 786440 | tf_op jit(solution)/shard_map/ppermute | solution.py:450
  250.6 5.9 %collective-permute-start.28 = (bf16[16,4096]{1,0:T(8,128)(2,1)S(1)}, bf16[16,4096]{1,0:T(8,128)(2,1)S(1)}, u32[]{:S(2)}, u32[]{:S(2)}) collective-permute-start(bf16[16,4096]{1,0:T(8,128)(2,1)S(1)} %slice.289), channel_id=1, source_target_pairs={{0,32},{1,97},{32,0},{33,65},{64,96},{65,33},{96,64},{97,1},{2,34}... | collective-permute-start | bytes 393224 | tf_op jit(solution)/shard_map/ppermute | solution.py:450
  252.1 6.9 %collective-permute-start.19 = (bf16[16,4096]{1,0:T(8,128)(2,1)S(1)}, bf16[16,4096]{1,0:T(8,128)(2,1)S(1)}, u32[]{:S(2)}, u32[]{:S(2)}) collective-permute-start(bf16[16,4096]{1,0:T(8,128)(2,1)S(1)} %slice.277), channel_id=1, source_target_pairs={{0,2},{1,7},{2,0},{3,5},{4,6},{5,3},{6,4},{7,1},{8,10},{9,15},{10,... | collective-permute-start | bytes 393224 | tf_op jit(solution)/shard_map/ppermute | solution.py:450
  256.4 5.0 %collective-permute-start.10 = (bf16[16,4096]{1,0:T(8,128)(2,1)S(1)}, bf16[16,4096]{1,0:T(8,128)(2,1)S(1)}, u32[]{:S(2)}, u32[]{:S(2)}) collective-permute-start(bf16[16,4096]{1,0:T(8,128)(2,1)S(1)} %slice.265), channel_id=1, source_target_pairs={{0,8},{1,25},{8,0},{9,17},{16,24},{17,9},{24,16},{25,1},{2,10},{3,... | collective-permute-start | bytes 393224 | tf_op jit(solution)/shard_map/ppermute | solution.py:450
  257.2 7.4 %collective-permute-start.29 = (bf16[8,4096]{1,0:T(8,128)(2,1)S(1)}, bf16[8,4096]{1,0:T(8,128)(2,1)S(1)}, u32[]{:S(2)}, u32[]{:S(2)}) collective-permute-start(bf16[8,4096]{1,0:T(8,128)(2,1)S(1)} %get-tuple-element.101), channel_id=1, source_target_pairs={{0,96},{1,33},{32,64},{33,1},{64,32},{65,97},{96,0},{97,65},{2,98}... | collective-permute-start | bytes 196616 | tf_op jit(solution)/shard_map/ppermute | solution.py:450
  259.6 5.5 %collective-permute-start.20 = (bf16[8,4096]{1,0:T(8,128)(2,1)S(1)}, bf16[8,4096]{1,0:T(8,128)(2,1)S(1)}, u32[]{:S(2)}, u32[]{:S(2)}) collective-permute-start(bf16[8,4096]{1,0:T(8,128)(2,1)S(1)} %get-tuple-element.103), channel_id=1, source_target_pairs={{0,6},{1,3},{2,4},{3,1},{4,2},{5,7},{6,0},{7,5},{8,14},{9,11},{10,... | collective-permute-start | bytes 196616 | tf_op jit(solution)/shard_map/ppermute | solution.py:450
  262.1 5.5 %collective-permute-start.11 = (bf16[8,4096]{1,0:T(8,128)(2,1)S(1)}, bf16[8,4096]{1,0:T(8,128)(2,1)S(1)}, u32[]{:S(2)}, u32[]{:S(2)}) collective-permute-start(bf16[8,4096]{1,0:T(8,128)(2,1)S(1)} %get-tuple-element.105), channel_id=1, source_target_pairs={{0,24},{1,9},{8,16},{9,1},{16,8},{17,25},{24,0},{25,17},{2,26},{3,... | collective-permute-start | bytes 196616 | tf_op jit(solution)/shard_map/ppermute | solution.py:450
  264.6 3.0 %copy-start.26 = (bf16[8,4096]{1,0:T(8,128)(2,1)}, bf16[8,4096]{1,0:T(8,128)(2,1)S(1)}, u32[]{:S(2)}) copy-start(bf16[8,4096]{1,0:T(8,128)(2,1)S(1)} %collective-permute-done.29.refs_2_) | copy-start | bytes 196612
  265.1 2.5 copy-start.27
  267.6 0.6 copy-start.28
Sparse Core Ops, SparseCore 0:
  11.7 95.5 all-gather.1
where the time goes:
time: 283 us; the launch traced here: 278 us
  waiting for transfers between devices  110 us (39%)
  Pallas kernels  71.6 us (25%)
  starting transfers between devices  39.1 us (14%)
  other arithmetic  34.1 us (12%)
  between operations  14.7 us (5%)
  local copies, waits for them, and re-layouts  9 us (3%)
    all_gather x1, waiting for transfers between devices, body(): weights = lax.all_gather(shard, ALL, axis=0, tiled=True)  76.4 us
    pallas_call x9, Pallas kernels, run(): pl.pallas_call(with_order, out_shape=tuple(out_shape) + tuple((arr(t.shap...  71.6 us
    ppermute x24, starting transfers between devices, to_partner(): return lax.ppermute(a, (axis, 'c'), pairs)  35.6 us
    ppermute x24, waiting for transfers between devices, to_partner(): return lax.ppermute(a, (axis, 'c'), pairs)  28.9 us
    add x24, other arithmetic, added(): total = total + a  22.4 us
  transfers between devices with their start and end apart: 31, of which 14 were waited for; matrix products, arithmetic and copies ran while one was open for 14% of the time, Pallas kernels for 12%

commit v1 on v0

--- a/solution.py
+++ b/solution.py
@@ -428,7 +428,7 @@
     return (1, 3) if core == 0 else (3, 1)
 
 
-def row_features(order):
+def row_features(order, swapped=False):
     core = lax.axis_index("c")
     row = jnp.arange(D, dtype=jnp.int32)
     mine, inner = row >= ROWS, row % ROWS
@@ -436,7 +436,8 @@
     place = {}
     for axis, size in zip(order, (128, 32, 8)):
         turn = inner // size % 4
-        apart = jnp.where(turn == 0, 2, jnp.where(turn == 3, 0, jnp.where((turn == 1) == (side == 0), 1, 3)))
+        low = side == (1 if swapped and axis == order[0] else 0)
+        apart = jnp.where(turn == 0, 2, jnp.where(turn == 3, 0, jnp.where((turn == 1) == low, 1, 3)))
         place[axis] = lax.axis_index(axis) ^ apart
     return ((place["y"] * 4 + place["z"]) * 4 + place["x"]) * 16 + side * 8 + inner % 8
 
@@ -445,8 +446,8 @@
     return (row_features(order)[:, None] == jnp.arange(D, dtype=jnp.int32)[None, :]).astype(bf16)
 
 
-def to_partner(a, axis, step):
-    pairs = [(i * 2 + c, (i ^ hops(c)[step]) * 2 + c) for i in range(4) for c in range(2)]
+def to_partner(a, axis, step, swapped=0):
+    pairs = [(i * 2 + c, (i ^ hops(c ^ swapped)[step]) * 2 + c) for i in range(4) for c in range(2)]
     return lax.ppermute(a, (axis, "c"), pairs)
 
 
@@ -462,8 +463,8 @@
 
 
 class PartSum:
-    def __init__(self, order, sib, own):
-        self.axis = order[0]
+    def __init__(self, order, sib, own, swapped=0):
+        self.axis, self.swapped = order[0], swapped
         self.own, self.arrived = own, to_sibling(sib)
         self.lo, self.step, self.got = 0, 0, None
 
@@ -477,7 +478,7 @@
     def send(self):
         rows = (ROWS - self.lo) // 2
         out = self.piece(self.lo, rows)
-        got = to_partner(out, self.axis, self.step)
+        got = to_partner(out, self.axis, self.step, self.swapped)
         self.got = got if self.got is None else (got, self.got)
         self.lo += rows
         self.step += 1
@@ -509,6 +510,7 @@
     wide = arr((n, D), f32)
     vm = pltpu.VMEM
     orders = jnp.concatenate([row_features(order)[::8] for order in ORDERS])
+    att_orders = jnp.concatenate([row_features(order, True)[::8] for order in ORDERS])
     gt, *gtts = run(
         cotangent_kernel, "cotangent", (cotangent, seg_col, *perms),
         (tile,) + (arr((D, n), bf16),) * CHUNKS,
@@ -544,7 +546,7 @@
         after += (f.send(),)
     block_output, input_grad, *pieces = run(
         back_kernel, "back",
-        (gains, seg_col, cos, sin, gt, residual, branch, gh2, qkv, probs, h1, mixed, tokens, weights, orders),
+        (gains, seg_col, cos, sin, gt, residual, branch, gh2, qkv, probs, h1, mixed, tokens, weights, att_orders),
         (tile, wide) + (arr((ROWS, A_COLS), bf16),) * 6,
         [vm((n, D), f32)] * 3
         + [vm((n, 3 * D), bf16), vm((H, n, n), f32)]
@@ -561,7 +563,7 @@
     )
     for f, own in zip(ff, pieces[6:]):
         f.own = own
-    att = [part_sum(ORDERS[j], pieces[j], pieces[3 + j]) for j in range(CHUNKS)]
+    att = [part_sum(ORDERS[j], pieces[j], pieces[3 + j], 1) for j in range(CHUNKS)]
     return block_output, input_grad, ff, att
 
 

time: 283 us -> 280 us (0.989)
  the two profiles are of different devices: /device:TPU:0 before, /device:TPU:2 now
where the time goes in v1:
time: 280 us; the launch traced here: 276 us
  waiting for transfers between devices  98.5 us (35%)
  Pallas kernels  71.5 us (26%)
  starting transfers between devices  41 us (15%)
  other arithmetic  39.8 us (14%)
  between operations  14.7 us (5%)
  local copies, waits for them, and re-layouts  10.3 us (4%)
    all_gather x1, waiting for transfers between devices, body(): weights = lax.all_gather(shard, ALL, axis=0, tiled=True)  74.5 us
    pallas_call x9, Pallas kernels, run(): pl.pallas_call(with_order, out_shape=tuple(out_shape) + tuple((arr(t.shap...  71.5 us
    ppermute x24, starting transfers between devices, to_partner(): return lax.ppermute(a, (axis, 'c'), pairs)  37.8 us
    add x24, other arithmetic, added(): total = total + a  25.6 us
    ppermute x24, waiting for transfers between devices, to_partner(): return lax.ppermute(a, (axis, 'c'), pairs)  19.8 us
  transfers between devices with their start and end apart: 31, of which 11 were waited for; matrix products, arithmetic and copies ran while one was open for 17% of the time, Pallas kernels for 12%

profile of v1, /device:TPU:2, one launch (start us, length us, event | category | flops | bytes accessed | tf_op | source)
XLA Modules:
  0.0 275.7 jit_solution(2535804424651337587)
XLA Ops:
  7.2 0.7 pad_maximum_fusion.2
  8.6 1.7 pack.1
  11.0 1.7 fusion.refs_2_
  12.8 1.8 fusion.1.refs_3_
  14.5 1.7 fusion.2.refs_4_
  17.2 1.3 add_select_fusion.refs_1_
  18.6 6.0 %cotangent.1 = (bf16[256,1024]{1,0:T(8,128)(2,1)}, bf16[1024,256]{1,0:T(8,128)(2,1)}, bf16[1024,256]{1,0:T(8,128)(2,1)}, bf16[1024,256]{1,0:T(8,128)(2,1)}) custom-call(bf16[256,1024]{1,0:T(8,128)(2,1)} %refs_0_.5, s32[256,1]{1,0:T(8,128)} %add_select_fusion.refs_1_, bf16[1024,1024]{1,0:T(8,128)(2,1)} %fusion.refs_2_, bf16[1024,1024]{1,0:T(8,128)(2,1)} %fusion.1.refs_3_, ...), custom_call_target="tpu_custom_call" | custom-call | flops 100000000376832 | bytes 1024 | tf_op jit(solution)/shard_map/cotangent/pallas_call | solution.py:381
  24.6 0.9 slice.200
  25.5 0.9 slice.201
  26.4 0.9 slice.202
  27.9 0.7 select_reduce_fusion
  29.8 1.0 pad_maximum_fusion
  30.8 1.9 compare_select_fusion.refs_2_
  32.7 74.5 %all-gather.2.cloned.1.call-done.refs_5_.refs_6_.refs_13_ = bf16[1024,12288]{1,0:T(8,128)(2,1)} async-done(((bf16[8,12288]{1,0:T(8,128)(2,1)}), bf16[1024,12288]{1,0:T(8,128)(2,1)}) %all-gather.2.cloned.1.call-update) | async-done | bytes 25165840 | tf_op jit(solution)/shard_map/all_gather | solution.py:615
  107.2 10.9 %attend.1 = (bf16[256,3072]{1,0:T(8,128)(2,1)}, f32[16,256,256]{2,1,0:T(8,128)}, f32[256,1024]{1,0:T(8,128)}, bf16[256,1024]{1,0:T(8,128)(2,1)}, bf16[256,1024]{...) custom-call(bf16[256,1024]{1,0:T(8,128)(2,1)} %refs_12_.1, s32[256,1]{1,0:T(8,128)} %add_select_fusion.refs_1_, ...), custom_call_target="tpu_custom_call" | custom-call | flops 100000000376832 | bytes 1024 | tf_op jit(solution)/shard_map/attend/pallas_call | solution.py:381
  118.2 23.2 %gated.1 = (f32[256,1024]{1,0:T(8,128)}, f32[256,1024]{1,0:T(8,128)}, bf16[512,2688]{1,0:T(8,128)(2,1)}, bf16[512,2688]{1,0:T(8,128)(2,1)}, bf16[512,2688]{1,0:T...) custom-call(s32[384]{0:T(512)} %pad_add_fusion.refs_0_, ...), custom_call_target="tpu_custom_call" | custom-call | flops 100000000376832 | bytes 1024 | tf_op jit(solution)/shard_map/gated/pallas_call | solution.py:381
  142.3 0.9 slice.203
  144.2 4.1 %collective-permute-done = bf16[512,2688]{1,0:T(8,128)(2,1)S(1)} collective-permute-done((bf16[512,2688]{1,0:T(8,128)(2,1)}, bf16[512,2688]{1,0:T(8,128)(2,1)S(1)}, u32[]{:S(2)}, u32[]{:S(2)}) %collective-permute-start) | collective-permute-done | bytes 2752544 | tf_op jit(solution)/shard_map/ppermute | solution.py:455
  148.4 3.6 %slice_add_fusion.2.refs_15_ = bf16[256,2688]{1,0:T(8,128)(2,1)} fusion(bf16[512,2688]{1,0:T(8,128)(2,1)S(1)} %collective-permute-done, bf16[512,2688]{1,0:T(8,128)(2,1)} %get-tuple-element.67.refs_18_), kind=kLoop, calls=%fused_computation.8 | loop fusion | flops 688128 | bytes 4128768 | tf_op jit(solution)/shard_map/add | solution.py:461
  151.9 0.7 collective-permute-start.4
  152.6 2.8 %slice_add_fusion.1.refs_16_ = bf16[256,2688]{1,0:T(8,128)(2,1)} fusion(bf16[512,2688]{1,0:T(8,128)(2,1)} %collective-permute-done.1, bf16[512,2688]{1,0:T(8,128)(2,1)S(1)} %copy-done.3), kind=kLoop, calls=%fused_computation.7 | loop fusion | flops 688128 | bytes 4128768 | tf_op jit(solution)/shard_map/add | solution.py:461
  155.4 1.4 collective-permute-start.13
  156.8 2.7 slice_add_fusion.refs_17_
  159.4 9.5 %collective-permute-start.22 = (bf16[256,2688]{1,0:T(8,128)(2,1)}, bf16[256,2688]{1,0:T(8,128)(2,1)}, u32[]{:S(2)}, u32[]{:S(2)}) collective-permute-start(bf16[256,2688]{1,0:T(8,128)(2,1)} %slice_add_fusion.refs_17_), channel_id=1, source_target_pairs={{0,8},{1,25},{8,0},{9,17},{16,24},{17,9},{24,16},{25,1},{2,10},{3,... | collective-permute-start | bytes 4128776 | tf_op jit(solution)/shard_map/ppermute | solution.py:451
  168.9 19.9 %back.1 = (bf16[256,1024]{1,0:T(8,128)(2,1)}, f32[256,1024]{1,0:T(8,128)}, bf16[512,1408]{1,0:T(8,128)(2,1)}, bf16[512,1408]{1,0:T(8,128)(2,1)}, bf16[512,1408]{...) custom-call(f32[8,1024]{1,0:T(8,128)} %get-tuple-element.54.refs_0_,, ...), custom_call_target="tpu_custom_call", output_to_operand_aliasing={{8}: (18, {}), {9}: (19, {}), {10}: (20, {})} | custom-call | flops 100000000376832 | bytes 1024 | tf_op jit(solution)/shard_map/back/pallas_call | solution.py:381
  188.8 1.6 collective-permute-start.21
  191.0 1.8 slice_add_fusion.7
  192.8 2.4 collective-permute-start.23
  195.3 1.7 slice_add_fusion.11
  197.7 1.3 slice_add_fusion.15
  199.0 0.8 collective-permute-start.5
  199.9 2.0 collective-permute-start.24
  201.9 1.7 collective-permute-start.15
  203.8 1.3 collective-permute-done.23
  205.1 0.7 collective-permute-start.6
  205.7 2.5 slice_add_fusion.6.refs_0_
  208.3 1.0 collective-permute-done.14
  209.3 2.5 slice_add_fusion.10.refs_0_
  211.8 2.1 slice_add_fusion.14.refs_0_
  214.1 2.9 %collective-permute-done.15.refs_4_ = bf16[256,1408]{1,0:T(8,128)(2,1)S(1)} collective-permute-done((bf16[256,1408]{1,0:T(8,128)(2,1)S(1)}, bf16[256,1408]{1,0:T(8,128)(2,1)S(1)}, u32[]{:S(2)}, u32[]{:S(2)}) %collective-permute-start.15) | collective-permute-done | bytes 720928 | tf_op jit(solution)/shard_map/ppermute | solution.py:451
  217.0 0.9 slice_add_fusion.20
  217.9 0.9 slice_add_fusion.22
  218.9 2.7 collective-permute-start.7
  221.6 0.8 copy-done.21
  222.4 2.6 turn.5
  225.0 2.1 collective-permute-start.26
  227.1 2.6 turn.4
  229.8 2.7 turn.3
  232.5 2.1 collective-permute-done.26
  234.6 1.2 add.576
  235.8 0.8 collective-permute-start.27
  236.6 2.7 collective-permute-done.17
  239.2 1.2 add.565
  240.4 1.8 collective-permute-start.18
  242.4 1.9 collective-permute-start.9
  244.5 3.6 %collective-permute-done.18 = bf16[32,4096]{1,0:T(8,128)(2,1)S(1)} collective-permute-done((bf16[32,4096]{1,0:T(8,128)(2,1)S(1)}, bf16[32,4096]{1,0:T(8,128)(2,1)S(1)}, u32[]{:S(2)}, u32[]{:S(2)}) %collective-permute-start.18) | collective-permute-done | bytes 262176 | tf_op jit(solution)/shard_map/ppermute | solution.py:451
  248.6 1.4 collective-permute-done.9
  250.1 3.3 %collective-permute-start.10 = (bf16[16,4096]{1,0:T(8,128)(2,1)S(1)}, bf16[16,4096]{1,0:T(8,128)(2,1)S(1)}, u32[]{:S(2)}, u32[]{:S(2)}) collective-permute-start(bf16[16,4096]{1,0:T(8,128)(2,1)S(1)} %slice.277), channel_id=1, source_target_pairs={{0,8},{1,25},{8,0},{9,17},{16,24},{17,9},{24,16},{25,1},{2,10},{3,... | collective-permute-start | bytes 393224 | tf_op jit(solution)/shard_map/ppermute | solution.py:451
  254.0 2.5 collective-permute-start.29
  257.2 1.6 collective-permute-start.20
  260.1 1.3 collective-permute-done.20.refs_1_
  261.5 3.5 %collective-permute-done.11.refs_0_ = bf16[8,4096]{1,0:T(8,128)(2,1)S(1)} collective-permute-done((bf16[8,4096]{1,0:T(8,128)(2,1)S(1)}, bf16[8,4096]{1,0:T(8,128)(2,1)S(1)}, u32[]{:S(2)}, u32[]{:S(2)}) %collective-permute-start.11) | collective-permute-done | bytes 65568 | tf_op jit(solution)/shard_map/ppermute | solution.py:451
  265.6 1.8 finish.1
  267.4 1.3 slice_bitcast_fusion
  (129 shorter events, 12.2 us)
Async XLA Ops:
  7.2 100.1 %all-gather.2.cloned.1.call-start = ((), (), s32[]{:S(2)}) async-start(), calls=%async_computation | async-start | bytes 25362432 | tf_op jit(solution)/shard_map/all_gather | solution.py:615
  10.4 4.1 %copy-start.18 = (s32[1024]{0:T(1024)}, s32[1024]{0:T(1024)S(1)}, u32[]{:S(2)}) copy-start(s32[1024]{0:T(1024)S(1)} %get-tuple-element.114) | copy-start | bytes 12292
  10.4 4.1 %copy-start.19 = (s32[1024]{0:T(1024)}, s32[1024]{0:T(1024)S(1)}, u32[]{:S(2)}) copy-start(s32[1024]{0:T(1024)S(1)} %get-tuple-element.113) | copy-start | bytes 12292
  11.0 3.5 %copy-start.17 = (s32[1024]{0:T(1024)}, s32[1024]{0:T(1024)S(1)}, u32[]{:S(2)}) copy-start(s32[1024]{0:T(1024)S(1)} %get-tuple-element.115) | copy-start | bytes 12292
  12.8 3.5 %copy-start.25 = (s32[4]{0:T(128)S(1)}, s32[4]{0:T(128)}, u32[]{:S(2)}) copy-start(s32[4]{0:T(128)} %param.16) | copy-start | bytes 52
  16.4 0.7 copy-start.27
  17.1 7.5 %copy-start.20 = (s32[256]{0:T(256)}, s32[256]{0:T(256)S(1)}, u32[]{:S(2)}) copy-start(s32[256]{0:T(256)S(1)} %convert_reduce_fusion) | copy-start | bytes 3076
  18.6 9.3 %copy-start.26 = (s32[4]{0:T(128)S(1)}, s32[4]{0:T(128)}, u32[]{:S(2)}) copy-start(s32[4]{0:T(128)} %param.16) | copy-start | bytes 52
  18.6 9.3 %copy-start.28 = (s32[4,1]{0,1:T(1,128)S(1)}, s32[4,1]{0,1:T(1,128)}, u32[]{:S(2)}) copy-start(s32[4,1]{0,1:T(1,128)} %copy-done.27) | copy-start | bytes 52
  141.4 7.0 %collective-permute-start = (bf16[512,2688]{1,0:T(8,128)(2,1)}, bf16[512,2688]{1,0:T(8,128)(2,1)S(1)}, u32[]{:S(2)}, u32[]{:S(2)}) collective-permute-start(bf16[512,2688]{1,0:T(8,128)(2,1)} %get-tuple-element.68), channel_id=1, source_target_pairs={{0,1},{1,0},{2,3},{3,2},{4,5},{5,4},{6,7},{7,6},{8,9},{9,8},{10,11... | collective-permute-start | bytes 8257544 | tf_op jit(solution)/shard_map/ppermute | solution.py:455
  141.8 10.8 %collective-permute-start.1 = (bf16[512,2688]{1,0:T(8,128)(2,1)}, bf16[512,2688]{1,0:T(8,128)(2,1)}, u32[]{:S(2)}, u32[]{:S(2)}) collective-permute-start(bf16[512,2688]{1,0:T(8,128)(2,1)} %get-tuple-element.71), channel_id=1, source_target_pairs={{0,1},{1,0},{2,3},{3,2},{4,5},{5,4},{6,7},{7,6},{8,9},{9,8},{10,11... | collective-permute-start | bytes 8257544 | tf_op jit(solution)/shard_map/ppermute | solution.py:455
  142.0 14.8 %collective-permute-start.2 = (bf16[512,2688]{1,0:T(8,128)(2,1)}, bf16[512,2688]{1,0:T(8,128)(2,1)}, u32[]{:S(2)}, u32[]{:S(2)}) collective-permute-start(bf16[512,2688]{1,0:T(8,128)(2,1)} %get-tuple-element.74), channel_id=1, source_target_pairs={{0,1},{1,0},{2,3},{3,2},{4,5},{5,4},{6,7},{7,6},{8,9},{9,8},{10,11... | collective-permute-start | bytes 8257544 | tf_op jit(solution)/shard_map/ppermute | solution.py:455
  143.6 9.0 %copy-start.3 = (bf16[512,2688]{1,0:T(8,128)(2,1)S(1)}, bf16[512,2688]{1,0:T(8,128)(2,1)}, u32[]{:S(2)}) copy-start(bf16[512,2688]{1,0:T(8,128)(2,1)} %get-tuple-element.70.refs_19_) | copy-start | bytes 8257540
  148.4 7.0 %copy-start = (bf16[512,2688]{1,0:T(8,128)(2,1)}, bf16[512,2688]{1,0:T(8,128)(2,1)S(1)}, u32[]{:S(2)}) copy-start(bf16[512,2688]{1,0:T(8,128)(2,1)S(1)} %collective-permute-done) | copy-start | bytes 8257540
  151.9 4.8 %copy-start.4 = (bf16[512,2688]{1,0:T(8,128)(2,1)S(1)}, bf16[512,2688]{1,0:T(8,128)(2,1)}, u32[]{:S(2)}) copy-start(bf16[512,2688]{1,0:T(8,128)(2,1)} %get-tuple-element.73.refs_20_) | copy-start | bytes 8257540
  151.9 45.1 %collective-permute-start.4 = (bf16[256,2688]{1,0:T(8,128)(2,1)}, bf16[256,2688]{1,0:T(8,128)(2,1)}, u32[]{:S(2)}, u32[]{:S(2)}) collective-permute-start(bf16[256,2688]{1,0:T(8,128)(2,1)} %slice_add_fusion.2.refs_15_), channel_id=1, source_target_pairs={{0,2},{1,7},{2,0},{3,5},{4,6},{5,3},{6,4},{7,1},{8,10},{9,15},{10,... | collective-permute-start | bytes 4128776 | tf_op jit(solution)/shard_map/ppermute | solution.py:451
  155.4 37.4 %collective-permute-start.13 = (bf16[256,2688]{1,0:T(8,128)(2,1)}, bf16[256,2688]{1,0:T(8,128)(2,1)}, u32[]{:S(2)}, u32[]{:S(2)}) collective-permute-start(bf16[256,2688]{1,0:T(8,128)(2,1)} %slice_add_fusion.1.refs_16_), channel_id=1, source_target_pairs={{0,32},{1,97},{32,0},{33,65},{64,96},{65,33},{96,64},{97,1},{2,34}... | collective-permute-start | bytes 4128776 | tf_op jit(solution)/shard_map/ppermute | solution.py:451
  159.4 31.2 %collective-permute-start.22 = (bf16[256,2688]{1,0:T(8,128)(2,1)}, bf16[256,2688]{1,0:T(8,128)(2,1)}, u32[]{:S(2)}, u32[]{:S(2)}) collective-permute-start(bf16[256,2688]{1,0:T(8,128)(2,1)} %slice_add_fusion.refs_17_), channel_id=1, source_target_pairs={{0,8},{1,25},{8,0},{9,17},{16,24},{17,9},{24,16},{25,1},{2,10},{3,... | collective-permute-start | bytes 4128776 | tf_op jit(solution)/shard_map/ppermute | solution.py:451
  188.8 10.2 %collective-permute-start.21 = (bf16[512,1408]{1,0:T(8,128)(2,1)}, bf16[512,1408]{1,0:T(8,128)(2,1)S(1)}, u32[]{:S(2)}, u32[]{:S(2)}) collective-permute-start(bf16[512,1408]{1,0:T(8,128)(2,1)} %get-tuple-element.91), channel_id=1, source_target_pairs={{0,1},{1,0},{2,3},{3,2},{4,5},{5,4},{6,7},{7,6},{8,9},{9,8},{10,11... | collective-permute-start | bytes 4325384 | tf_op jit(solution)/shard_map/ppermute | solution.py:455
  190.3 9.5 %collective-permute-start.12 = (bf16[512,1408]{1,0:T(8,128)(2,1)}, bf16[512,1408]{1,0:T(8,128)(2,1)S(1)}, u32[]{:S(2)}, u32[]{:S(2)}) collective-permute-start(bf16[512,1408]{1,0:T(8,128)(2,1)} %get-tuple-element.85), channel_id=1, source_target_pairs={{0,1},{1,0},{2,3},{3,2},{4,5},{5,4},{6,7},{7,6},{8,9},{9,8},{10,11... | collective-permute-start | bytes 4325384 | tf_op jit(solution)/shard_map/ppermute | solution.py:455
  190.6 11.3 %collective-permute-start.3 = (bf16[512,1408]{1,0:T(8,128)(2,1)}, bf16[512,1408]{1,0:T(8,128)(2,1)S(1)}, u32[]{:S(2)}, u32[]{:S(2)}) collective-permute-start(bf16[512,1408]{1,0:T(8,128)(2,1)} %get-tuple-element.79), channel_id=1, source_target_pairs={{0,1},{1,0},{2,3},{3,2},{4,5},{5,4},{6,7},{7,6},{8,9},{9,8},{10,11... | collective-permute-start | bytes 4325384 | tf_op jit(solution)/shard_map/ppermute | solution.py:455
  191.0 6.7 %copy-start.2 = (bf16[512,2688]{1,0:T(8,128)(2,1)S(1)}, bf16[512,2688]{1,0:T(8,128)(2,1)}, u32[]{:S(2)}) copy-start(bf16[512,2688]{1,0:T(8,128)(2,1)} %get-tuple-element.80) | copy-start | bytes 8257540
  192.8 4.9 %copy-start.1 = (bf16[512,2688]{1,0:T(8,128)(2,1)S(1)}, bf16[512,2688]{1,0:T(8,128)(2,1)}, u32[]{:S(2)}) copy-start(bf16[512,2688]{1,0:T(8,128)(2,1)} %copy-done) | copy-start | bytes 8257540
  192.8 12.2 %collective-permute-start.23 = (bf16[128,2688]{1,0:T(8,128)(2,1)S(1)}, bf16[128,2688]{1,0:T(8,128)(2,1)S(1)}, u32[]{:S(2)}, u32[]{:S(2)}) collective-permute-start(bf16[128,2688]{1,0:T(8,128)(2,1)S(1)} %slice_add_fusion.7), channel_id=1, source_target_pairs={{0,24},{1,9},{8,16},{9,1},{16,8},{17,25},{24,0},{25,17},{2,26},{3,... | collective-permute-start | bytes 2064392 | tf_op jit(solution)/shard_map/ppermute | solution.py:451
  195.3 4.5 %copy-start.7 = (bf16[512,1408]{1,0:T(8,128)(2,1)S(1)}, bf16[512,1408]{1,0:T(8,128)(2,1)}, u32[]{:S(2)}) copy-start(bf16[512,1408]{1,0:T(8,128)(2,1)} %get-tuple-element.90.refs_1_) | copy-start | bytes 4325380
  197.0 4.8 %copy-start.6 = (bf16[512,1408]{1,0:T(8,128)(2,1)S(1)}, bf16[512,1408]{1,0:T(8,128)(2,1)}, u32[]{:S(2)}) copy-start(bf16[512,1408]{1,0:T(8,128)(2,1)} %get-tuple-element.84.refs_1_) | copy-start | bytes 4325380
  197.0 12.2 %collective-permute-start.14 = (bf16[128,2688]{1,0:T(8,128)(2,1)S(1)}, bf16[128,2688]{1,0:T(8,128)(2,1)S(1)}, u32[]{:S(2)}, u32[]{:S(2)}) collective-permute-start(bf16[128,2688]{1,0:T(8,128)(2,1)S(1)} %slice_add_fusion.11), channel_id=1, source_target_pairs={{0,96},{1,33},{32,64},{33,1},{64,32},{65,97},{96,0},{97,65},{2,98}... | collective-permute-start | bytes 2064392 | tf_op jit(solution)/shard_map/ppermute | solution.py:451
  199.0 4.7 %copy-start.5 = (bf16[512,1408]{1,0:T(8,128)(2,1)S(1)}, bf16[512,1408]{1,0:T(8,128)(2,1)}, u32[]{:S(2)}) copy-start(bf16[512,1408]{1,0:T(8,128)(2,1)} %get-tuple-element.78.refs_1_) | copy-start | bytes 4325380
  199.0 15.0 %copy-start.10 = (bf16[512,1408]{1,0:T(8,128)(2,1)}, bf16[512,1408]{1,0:T(8,128)(2,1)S(1)}, u32[]{:S(2)}) copy-start(bf16[512,1408]{1,0:T(8,128)(2,1)S(1)} %collective-permute-done.21.refs_2_) | copy-start | bytes 4325380
  199.0 12.8 %collective-permute-start.5 = (bf16[128,2688]{1,0:T(8,128)(2,1)S(1)}, bf16[128,2688]{1,0:T(8,128)(2,1)S(1)}, u32[]{:S(2)}, u32[]{:S(2)}) collective-permute-start(bf16[128,2688]{1,0:T(8,128)(2,1)S(1)} %slice_add_fusion.15), channel_id=1, source_target_pairs={{0,6},{1,3},{2,4},{3,1},{4,2},{5,7},{6,0},{7,5},{8,14},{9,11},{10,... | collective-permute-start | bytes 2064392 | tf_op jit(solution)/shard_map/ppermute | solution.py:451
  199.8 17.1 %copy-start.9 = (bf16[512,1408]{1,0:T(8,128)(2,1)}, bf16[512,1408]{1,0:T(8,128)(2,1)S(1)}, u32[]{:S(2)}) copy-start(bf16[512,1408]{1,0:T(8,128)(2,1)S(1)} %collective-permute-done.12.refs_2_) | copy-start | bytes 4325380
  199.9 14.1 %collective-permute-start.24 = (bf16[256,1408]{1,0:T(8,128)(2,1)S(1)}, bf16[256,1408]{1,0:T(8,128)(2,1)S(1)}, u32[]{:S(2)}, u32[]{:S(2)}) collective-permute-start(bf16[256,1408]{1,0:T(8,128)(2,1)S(1)} %slice_add_fusion.3), channel_id=1, source_target_pairs={{0,24},{1,9},{8,16},{9,1},{16,8},{17,25},{24,0},{25,17},{2,26},{3,... | collective-permute-start | bytes 2162696 | tf_op jit(solution)/shard_map/ppermute | solution.py:451
  201.9 15.9 %copy-start.8 = (bf16[512,1408]{1,0:T(8,128)(2,1)}, bf16[512,1408]{1,0:T(8,128)(2,1)S(1)}, u32[]{:S(2)}) copy-start(bf16[512,1408]{1,0:T(8,128)(2,1)S(1)} %collective-permute-done.3.refs_2_) | copy-start | bytes 4325380
  201.9 15.0 %collective-permute-start.15 = (bf16[256,1408]{1,0:T(8,128)(2,1)S(1)}, bf16[256,1408]{1,0:T(8,128)(2,1)S(1)}, u32[]{:S(2)}, u32[]{:S(2)}) collective-permute-start(bf16[256,1408]{1,0:T(8,128)(2,1)S(1)} %slice_add_fusion.4), channel_id=1, source_target_pairs={{0,96},{1,33},{32,64},{33,1},{64,32},{65,97},{96,0},{97,65},{2,98}... | collective-permute-start | bytes 2162696 | tf_op jit(solution)/shard_map/ppermute | solution.py:451
  205.1 12.8 %collective-permute-start.6 = (bf16[256,1408]{1,0:T(8,128)(2,1)S(1)}, bf16[256,1408]{1,0:T(8,128)(2,1)S(1)}, u32[]{:S(2)}, u32[]{:S(2)}) collective-permute-start(bf16[256,1408]{1,0:T(8,128)(2,1)S(1)} %slice_add_fusion.5), channel_id=1, source_target_pairs={{0,6},{1,3},{2,4},{3,1},{4,2},{5,7},{6,0},{7,5},{8,14},{9,11},{10,... | collective-permute-start | bytes 2162696 | tf_op jit(solution)/shard_map/ppermute | solution.py:451
  213.9 4.8 %copy-start.16 = (bf16[256,1408]{1,0:T(8,128)(2,1)}, bf16[256,1408]{1,0:T(8,128)(2,1)S(1)}, u32[]{:S(2)}) copy-start(bf16[256,1408]{1,0:T(8,128)(2,1)S(1)} %collective-permute-done.24.refs_4_) | copy-start | bytes 2162692
  214.0 7.6 %collective-permute-start.25 = (bf16[128,1408]{1,0:T(8,128)(2,1)S(1)}, bf16[128,1408]{1,0:T(8,128)(2,1)S(1)}, u32[]{:S(2)}, u32[]{:S(2)}) collective-permute-start(bf16[128,1408]{1,0:T(8,128)(2,1)S(1)} %slice_add_fusion.18), channel_id=1, source_target_pairs={{0,8},{1,25},{8,0},{9,17},{16,24},{17,9},{24,16},{25,1},{2,10},{3,... | collective-permute-start | bytes 1081352 | tf_op jit(solution)/shard_map/ppermute | solution.py:451
  217.0 4.6 %copy-start.15 = (bf16[256,1408]{1,0:T(8,128)(2,1)}, bf16[256,1408]{1,0:T(8,128)(2,1)S(1)}, u32[]{:S(2)}) copy-start(bf16[256,1408]{1,0:T(8,128)(2,1)S(1)} %collective-permute-done.15.refs_4_) | copy-start | bytes 2162692
  217.9 9.2 %collective-permute-start.16 = (bf16[128,1408]{1,0:T(8,128)(2,1)}, bf16[128,1408]{1,0:T(8,128)(2,1)}, u32[]{:S(2)}, u32[]{:S(2)}) collective-permute-start(bf16[128,1408]{1,0:T(8,128)(2,1)} %slice_add_fusion.20), channel_id=1, source_target_pairs={{0,32},{1,97},{32,0},{33,65},{64,96},{65,33},{96,64},{97,1},{2,34}... | collective-permute-start | bytes 1081352 | tf_op jit(solution)/shard_map/ppermute | solution.py:451
  217.9 1.0 copy-start.14
  218.9 10.8 %collective-permute-start.7 = (bf16[128,1408]{1,0:T(8,128)(2,1)}, bf16[128,1408]{1,0:T(8,128)(2,1)}, u32[]{:S(2)}, u32[]{:S(2)}) collective-permute-start(bf16[128,1408]{1,0:T(8,128)(2,1)} %slice_add_fusion.22), channel_id=1, source_target_pairs={{0,2},{1,7},{2,0},{3,5},{4,6},{5,3},{6,4},{7,1},{8,10},{9,15},{10,... | collective-permute-start | bytes 1081352 | tf_op jit(solution)/shard_map/ppermute | solution.py:451
  221.6 0.8 copy-start.21
  225.0 9.6 %collective-permute-start.26 = (bf16[64,4096]{1,0:T(8,128)(2,1)}, bf16[64,4096]{1,0:T(8,128)(2,1)}, u32[]{:S(2)}, u32[]{:S(2)}) collective-permute-start(bf16[64,4096]{1,0:T(8,128)(2,1)} %get-tuple-element.93), channel_id=1, source_target_pairs={{0,2},{1,7},{2,0},{3,5},{4,6},{5,3},{6,4},{7,1},{8,10},{9,15},{10,... | collective-permute-start | bytes 1572872 | tf_op jit(solution)/shard_map/ppermute | solution.py:451
  229.7 9.5 %collective-permute-start.17 = (bf16[64,4096]{1,0:T(8,128)(2,1)}, bf16[64,4096]{1,0:T(8,128)(2,1)}, u32[]{:S(2)}, u32[]{:S(2)}) collective-permute-start(bf16[64,4096]{1,0:T(8,128)(2,1)} %get-tuple-element.87), channel_id=1, source_target_pairs={{0,8},{1,25},{8,0},{9,17},{16,24},{17,9},{24,16},{25,1},{2,10},{3,... | collective-permute-start | bytes 1572872 | tf_op jit(solution)/shard_map/ppermute | solution.py:451
  229.7 4.8 %copy-start.11 = (bf16[64,4096]{1,0:T(8,128)(2,1)S(1)}, bf16[64,4096]{1,0:T(8,128)(2,1)}, u32[]{:S(2)}) copy-start(bf16[64,4096]{1,0:T(8,128)(2,1)} %get-tuple-element.94) | copy-start | bytes 1572868
  232.4 6.8 %copy-start.12 = (bf16[64,4096]{1,0:T(8,128)(2,1)S(1)}, bf16[64,4096]{1,0:T(8,128)(2,1)}, u32[]{:S(2)}) copy-start(bf16[64,4096]{1,0:T(8,128)(2,1)} %get-tuple-element.88) | copy-start | bytes 1572868
  232.4 9.8 %copy-start.13 = (bf16[64,4096]{1,0:T(8,128)(2,1)S(1)}, bf16[64,4096]{1,0:T(8,128)(2,1)}, u32[]{:S(2)}) copy-start(bf16[64,4096]{1,0:T(8,128)(2,1)} %get-tuple-element.82) | copy-start | bytes 1572868
  232.4 9.8 %collective-permute-start.8 = (bf16[64,4096]{1,0:T(8,128)(2,1)}, bf16[64,4096]{1,0:T(8,128)(2,1)S(1)}, u32[]{:S(2)}, u32[]{:S(2)}) collective-permute-start(bf16[64,4096]{1,0:T(8,128)(2,1)} %get-tuple-element.81), channel_id=1, source_target_pairs={{0,32},{1,97},{32,0},{33,65},{64,96},{65,33},{96,64},{97,1},{2,34}... | collective-permute-start | bytes 1572872 | tf_op jit(solution)/shard_map/ppermute | solution.py:451
  235.8 8.6 %collective-permute-start.27 = (bf16[32,4096]{1,0:T(8,128)(2,1)S(1)}, bf16[32,4096]{1,0:T(8,128)(2,1)S(1)}, u32[]{:S(2)}, u32[]{:S(2)}) collective-permute-start(bf16[32,4096]{1,0:T(8,128)(2,1)S(1)} %slice.299), channel_id=1, source_target_pairs={{0,6},{1,3},{2,4},{3,1},{4,2},{5,7},{6,0},{7,5},{8,14},{9,11},{10,... | collective-permute-start | bytes 786440 | tf_op jit(solution)/shard_map/ppermute | solution.py:451
  240.4 7.7 %collective-permute-start.18 = (bf16[32,4096]{1,0:T(8,128)(2,1)S(1)}, bf16[32,4096]{1,0:T(8,128)(2,1)S(1)}, u32[]{:S(2)}, u32[]{:S(2)}) collective-permute-start(bf16[32,4096]{1,0:T(8,128)(2,1)S(1)} %slice.287), channel_id=1, source_target_pairs={{0,24},{1,9},{8,16},{9,1},{16,8},{17,25},{24,0},{25,17},{2,26},{3,... | collective-permute-start | bytes 786440 | tf_op jit(solution)/shard_map/ppermute | solution.py:451
  242.4 7.7 %collective-permute-start.9 = (bf16[32,4096]{1,0:T(8,128)(2,1)S(1)}, bf16[32,4096]{1,0:T(8,128)(2,1)S(1)}, u32[]{:S(2)}, u32[]{:S(2)}) collective-permute-start(bf16[32,4096]{1,0:T(8,128)(2,1)S(1)} %slice.275), channel_id=1, source_target_pairs={{0,96},{1,33},{32,64},{33,1},{64,32},{65,97},{96,0},{97,65},{2,98}... | collective-permute-start | bytes 786440 | tf_op jit(solution)/shard_map/ppermute | solution.py:451
  244.4 9.0 %collective-permute-start.28 = (bf16[16,4096]{1,0:T(8,128)(2,1)S(1)}, bf16[16,4096]{1,0:T(8,128)(2,1)S(1)}, u32[]{:S(2)}, u32[]{:S(2)}) collective-permute-start(bf16[16,4096]{1,0:T(8,128)(2,1)S(1)} %slice.301), channel_id=1, source_target_pairs={{0,32},{1,97},{32,0},{33,65},{64,96},{65,33},{96,64},{97,1},{2,34}... | collective-permute-start | bytes 393224 | tf_op jit(solution)/shard_map/ppermute | solution.py:451
  248.1 8.4 %collective-permute-start.19 = (bf16[16,4096]{1,0:T(8,128)(2,1)S(1)}, bf16[16,4096]{1,0:T(8,128)(2,1)S(1)}, u32[]{:S(2)}, u32[]{:S(2)}) collective-permute-start(bf16[16,4096]{1,0:T(8,128)(2,1)S(1)} %slice.289), channel_id=1, source_target_pairs={{0,2},{1,7},{2,0},{3,5},{4,6},{5,3},{6,4},{7,1},{8,10},{9,15},{10,... | collective-permute-start | bytes 393224 | tf_op jit(solution)/shard_map/ppermute | solution.py:451
  250.1 8.7 %collective-permute-start.10 = (bf16[16,4096]{1,0:T(8,128)(2,1)S(1)}, bf16[16,4096]{1,0:T(8,128)(2,1)S(1)}, u32[]{:S(2)}, u32[]{:S(2)}) collective-permute-start(bf16[16,4096]{1,0:T(8,128)(2,1)S(1)} %slice.277), channel_id=1, source_target_pairs={{0,8},{1,25},{8,0},{9,17},{16,24},{17,9},{24,16},{25,1},{2,10},{3,... | collective-permute-start | bytes 393224 | tf_op jit(solution)/shard_map/ppermute | solution.py:451
  254.0 6.1 %collective-permute-start.29 = (bf16[8,4096]{1,0:T(8,128)(2,1)S(1)}, bf16[8,4096]{1,0:T(8,128)(2,1)S(1)}, u32[]{:S(2)}, u32[]{:S(2)}) collective-permute-start(bf16[8,4096]{1,0:T(8,128)(2,1)S(1)} %get-tuple-element.101), channel_id=1, source_target_pairs={{0,96},{1,33},{32,64},{33,1},{64,32},{65,97},{96,0},{97,65},{2,98}... | collective-permute-start | bytes 196616 | tf_op jit(solution)/shard_map/ppermute | solution.py:451
  257.2 4.3 %collective-permute-start.20 = (bf16[8,4096]{1,0:T(8,128)(2,1)S(1)}, bf16[8,4096]{1,0:T(8,128)(2,1)S(1)}, u32[]{:S(2)}, u32[]{:S(2)}) collective-permute-start(bf16[8,4096]{1,0:T(8,128)(2,1)S(1)} %get-tuple-element.103), channel_id=1, source_target_pairs={{0,6},{1,3},{2,4},{3,1},{4,2},{5,7},{6,0},{7,5},{8,14},{9,11},{10,... | collective-permute-start | bytes 196616 | tf_op jit(solution)/shard_map/ppermute | solution.py:451
  259.5 5.5 %collective-permute-start.11 = (bf16[8,4096]{1,0:T(8,128)(2,1)S(1)}, bf16[8,4096]{1,0:T(8,128)(2,1)S(1)}, u32[]{:S(2)}, u32[]{:S(2)}) collective-permute-start(bf16[8,4096]{1,0:T(8,128)(2,1)S(1)} %get-tuple-element.105), channel_id=1, source_target_pairs={{0,24},{1,9},{8,16},{9,1},{16,8},{17,25},{24,0},{25,17},{2,26},{3,... | collective-permute-start | bytes 196616 | tf_op jit(solution)/shard_map/ppermute | solution.py:451
  260.1 4.8 %copy-start.22 = (bf16[8,4096]{1,0:T(8,128)(2,1)}, bf16[8,4096]{1,0:T(8,128)(2,1)S(1)}, u32[]{:S(2)}) copy-start(bf16[8,4096]{1,0:T(8,128)(2,1)S(1)} %collective-permute-done.29.refs_2_) | copy-start | bytes 196612
  261.5 3.5 %copy-start.23 = (bf16[8,4096]{1,0:T(8,128)(2,1)}, bf16[8,4096]{1,0:T(8,128)(2,1)S(1)}, u32[]{:S(2)}) copy-start(bf16[8,4096]{1,0:T(8,128)(2,1)S(1)} %collective-permute-done.20.refs_1_) | copy-start | bytes 196612
  265.0 0.6 copy-start.24
Sparse Core Ops, SparseCore 0:
  11.7 95.5 all-gather.1
